TPU v7x, 32 devices: a whole 2x2x4 slice. The times are simulated.
32 devices in a mesh: ctx: 8 (over y, x, core), fsdp: 4 (over z).
Axes of the slice: x: 2, y: 2, z: 4, core: 2. Of those that a mesh axis runs over, the one named last changes fastest.
Arguments:
- tokens: bfloat16 [4, 1024, 1024], P('fsdp', 'ctx'), may hold values from -6 to 6
- encoder: bfloat16 [4, 512, 1024], P('fsdp', 'ctx'), may hold values from -6 to 6
- decoder_segments: int32 [4, 1024], P('fsdp', 'ctx'), may hold values from 0 to 3, never falling along the last dimension, each value on 1 to 897 neighbouring positions
- source_segments: int32 [4, 512], P('fsdp', 'ctx'), may hold values from 0 to 3, never falling along the last dimension, each value on 1 to 449 neighbouring positions
- attn_weight: bfloat16 [1024, 8192], P('fsdp'), may hold values from -4 to 4
- up_weight: bfloat16 [1024, 8192], P('fsdp'), may hold values from -0.1875 to 0.1875
- down_weight: bfloat16 [1024, 8192], P('fsdp'), may hold values from -0.0625 to 0.0625
- vector_params: float32 [21, 1024], replicated, may hold values from -1 to 2
- cotangent: bfloat16 [4, 1024, 1024], P('fsdp', 'ctx'), may hold values from -6 to 6
Outputs:
- mixed: bfloat16 [4, 1024, 1024], P('fsdp', 'ctx')
- grad_tokens: float32 [4, 1024, 1024], P('fsdp', 'ctx')
- grad_encoder: float32 [4, 512, 1024], P('fsdp', 'ctx')
- grad_attn: float32 [1024, 8192], P(('ctx', 'fsdp'))
- grad_up: float32 [1024, 8192], P(('ctx', 'fsdp'))
- grad_down: float32 [1024, 8192], P(('ctx', 'fsdp'))
- grad_vectors: float32 [21, 1024], replicated
Inputs may be any that keep to these rules, and one draw needn't show every extreme that they name: `decoder_segments`: segment numbers never fall along a sequence; each of the 4 numbers occurs in every sequence; one document of each sequence has exactly 897 tokens. Decoder document k attends to encoder document k. `source_segments`: as for the decoder; one document of each sequence has exactly 449 states.
All inputs are finite; a program needn't handle non-finite values.
Results may differ from a plain program's by a relative error of at most 0.02.
Values may be sent and summed in bfloat16 or wider, within the bound.
A program may use at most 384 MiB of HBM per device.

v0:
```python
import jax
import jax.numpy as jnp
from jax import lax
from jax.sharding import PartitionSpec as P

D = 1024
H = 16
HD = 64


EPS = 1e-05
NEG = -1e30


def passed_along(array, axis, by):
    size = lax.axis_size(axis)
    return lax.ppermute(array, axis, [(i, (i + by) % size) for i in range(size)])


def layer_norm(value, gain, shift):
    mean_row = jnp.mean(value, axis=-1, keepdims=True)
    centred = value - mean_row
    spread = jnp.mean(centred * centred, axis=-1, keepdims=True)
    return centred * lax.rsqrt(spread + EPS) * gain + shift


def norm_back(value, gain, shift, grad_in):
    _, pull = jax.vjp(layer_norm, value, gain, shift)
    return pull(grad_in)


def gelu_exact(value):
    return jax.nn.gelu(value, approximate=False)


def times_t(left, right):
    return lax.dot_general(
        left, right, (((1,), (1,)), ((), ())), preferred_element_type=jnp.float32
    )


def key_mask(query_seg, query_pos, key_seg, key_first, causal):
    allowed = query_seg[:, None] == key_seg[None, :]
    if causal:
        key_pos = key_first + jnp.arange(key_seg.shape[0], dtype=jnp.int32)
        allowed = allowed & (query_pos[:, None] >= key_pos[None, :])
    return allowed[:, None, :]


def fold_step(queries, query_seg, query_pos, causal, state_now, shard_piece, first_row):
    run_max, run_sum, accum_out = state_now
    key_rows, value_rows, key_seg = shard_piece
    piece_rows = key_rows.shape[0]
    per_head_queries = queries.reshape(queries.shape[0], H, HD)
    per_head_keys = key_rows.reshape(piece_rows, H, HD)
    per_head_values = value_rows.reshape(piece_rows, H, HD)
    scores = jnp.einsum(
        "sft,rft->sfr", per_head_queries, per_head_keys, preferred_element_type=jnp.float32
    ) * HD ** (-0.5)
    allowed = key_mask(query_seg, query_pos, key_seg, first_row, causal)
    scores = jnp.where(allowed, scores, NEG)
    new_max = jnp.maximum(run_max, jnp.max(scores, axis=-1))
    weights = jnp.where(allowed, jnp.exp(scores - new_max[..., None]), 0.0)
    run_sum = jnp.sum(weights, axis=-1)
    accum_out = jnp.einsum(
        "tna,anu->tnu",
        weights.astype(jnp.bfloat16),
        per_head_values,
        preferred_element_type=jnp.float32,
    )
    return (new_max, run_sum, accum_out)


def block_back(
    queries,
    grad_out,
    log_total,
    row_delta,
    query_seg,
    query_pos,
    causal,
    key_rows,
    value_rows,
    key_seg,
    key_first,
):
    piece_rows = key_rows.shape[0]
    query_rows = queries.shape[0]
    scale = HD ** (-0.5)
    per_head_queries = queries.reshape(query_rows, H, HD)
    head_gradient = grad_out.reshape(query_rows, H, HD)
    per_head_keys = key_rows.reshape(piece_rows, H, HD)
    per_head_values = value_rows.reshape(piece_rows, H, HD)
    scores = (
        jnp.einsum(
            "sft,rft->sfr", per_head_queries, per_head_keys, preferred_element_type=jnp.float32
        )
        * scale
    )
    allowed = key_mask(query_seg, query_pos, key_seg, key_first, causal)
    softmax_weights = jnp.where(allowed, jnp.exp(scores - log_total[..., None]), 0.0)
    grad_value = jnp.einsum(
        "xqy,xqg->yqg",
        softmax_weights.astype(jnp.bfloat16),
        head_gradient,
        preferred_element_type=jnp.float32,
    )
    grad_prob = jnp.einsum(
        "sft,rft->sfr", head_gradient, per_head_values, preferred_element_type=jnp.float32
    )
    score_gradient = (softmax_weights * (grad_prob - row_delta[..., None]) * scale).astype(
        jnp.bfloat16
    )
    grad_query = jnp.einsum(
        "tna,anu->tnu", score_gradient, per_head_keys, preferred_element_type=jnp.float32
    )
    grad_key = jnp.einsum(
        "xqy,xqg->yqg", score_gradient, per_head_queries, preferred_element_type=jnp.float32
    )
    return (
        grad_query.reshape(query_rows, H * HD),
        grad_key.reshape(piece_rows, H * HD),
        grad_value.reshape(piece_rows, H * HD),
    )


def cycle_back(
    queries,
    grad_out,
    log_total,
    row_delta,
    query_seg,
    query_pos,
    causal,
    key_rows,
    value_rows,
    key_seg,
):
    cycle_size = lax.axis_size("ctx")
    own_index = lax.axis_index("ctx")
    piece_rows = key_rows.shape[0]

    def turn(turn_index, state_now):
        grad_query, blocks_now, grads_now = state_now
        owner_index = (own_index - turn_index) % cycle_size
        part_query, part_key, part_value = block_back(
            queries,
            grad_out,
            log_total,
            row_delta,
            query_seg,
            query_pos,
            causal,
            blocks_now[0],
            blocks_now[1],
            blocks_now[2],
            owner_index * piece_rows,
        )
        grads_now = (grads_now[0] + part_key, grads_now[1] + part_value)
        blocks_now = passed_along((blocks_now[0], blocks_now[1], blocks_now[2]), "ctx", 1)
        grads_now = (
            passed_along(grads_now[0].astype(jnp.bfloat16), "ctx", 1).astype(jnp.float32),
            passed_along(grads_now[1].astype(jnp.bfloat16), "ctx", 1).astype(jnp.float32),
        )
        return (grad_query + part_query, blocks_now, grads_now)

    empty_rows = jnp.zeros((piece_rows, key_rows.shape[1]), jnp.float32)
    start_state = (
        jnp.zeros(queries.shape, jnp.float32),
        (key_rows, value_rows, key_seg),
        (empty_rows, empty_rows),
    )
    grad_query, _, grads_home = lax.fori_loop(0, cycle_size, turn, start_state)
    return (grad_query, grads_home[0], grads_home[1])


def column_sum(value):
    return jnp.sum(value.astype(jnp.float32), axis=0)


def body(
    tokens,
    encoder,
    decoder_segments,
    source_segments,
    attn_weight,
    up_weight,
    down_weight,
    vector_params,
    cotangent,
):
    bfloat = jnp.bfloat16
    single = jnp.float32
    stream = tokens[0].astype(single)
    source = encoder[0]
    row_count = stream.shape[0]
    query_seg = decoder_segments[0].astype(bfloat)
    source_seg = source_segments[0].astype(bfloat)
    query_pos = lax.axis_index("ctx") * row_count + jnp.arange(row_count, dtype=jnp.int32)
    (
        gain_self,
        shift_self,
        gain_cross,
        shift_cross,
        gain_feed,
        shift_feed,
        bias_query,
        bias_value,
        bias_output,
        cross_query,
        cross_value,
        cross_output,
        bias_down,
    ) = [vector_params[row_index] for row_index in range(13)]
    bias_up = vector_params[13:].reshape(-1)
    zero_bias = jnp.zeros((D,), single)
    weights = lax.all_gather(attn_weight, "fsdp", axis=0, tiled=True)
    normed_self = layer_norm(stream, gain_self, shift_self).astype(bfloat)
    qkv_self = (
        jnp.dot(normed_self, weights[:, : 3 * D], preferred_element_type=single)
        + jnp.concatenate([bias_query, zero_bias, bias_value])
    ).astype(bfloat)
    query_self = qkv_self[:, :D]
    key_self = qkv_self[:, D : 2 * D]
    value_self = qkv_self[:, 2 * D :]
    start_state = (
        jnp.full((row_count, H), NEG, single),
        jnp.zeros((row_count, H), single),
        jnp.zeros((row_count, H, HD), single),
    )
    max_self, sum_self, accum_self = fold_step(
        query_self,
        query_seg,
        query_pos,
        True,
        start_state,
        (
            lax.all_gather(key_self, "ctx", axis=0, tiled=True),
            lax.all_gather(value_self, "ctx", axis=0, tiled=True),
            lax.all_gather(query_seg, "ctx", axis=0, tiled=True),
        ),
        jnp.int32(0),
    )
    heads_self = (accum_self / sum_self[..., None]).reshape(row_count, D)
    total_self = max_self + jnp.log(sum_self)
    heads_self_low = heads_self.astype(bfloat)
    after_self = (
        stream
        + jnp.dot(heads_self_low, weights[:, 3 * D : 4 * D], preferred_element_type=single)
        + bias_output
    )
    normed_cross = layer_norm(after_self, gain_cross, shift_cross).astype(bfloat)
    query_cross = (
        jnp.dot(normed_cross, weights[:, 4 * D : 5 * D], preferred_element_type=single)
        + cross_query
    ).astype(bfloat)
    kv_cross = (
        jnp.dot(source, weights[:, 5 * D : 7 * D], preferred_element_type=single)
        + jnp.concatenate([zero_bias, cross_value])
    ).astype(bfloat)
    key_cross = kv_cross[:, :D]
    value_cross = kv_cross[:, D:]
    max_cross, sum_cross, accum_cross = fold_step(
        query_cross,
        query_seg,
        query_pos,
        False,
        start_state,
        (
            lax.all_gather(key_cross, "ctx", axis=0, tiled=True),
            lax.all_gather(value_cross, "ctx", axis=0, tiled=True),
            lax.all_gather(source_seg, "ctx", axis=0, tiled=True),
        ),
        jnp.int32(0),
    )
    heads_cross = (accum_cross / sum_cross[..., None]).reshape(row_count, D)
    total_cross = max_cross + jnp.log(sum_cross)
    heads_cross_low = heads_cross.astype(bfloat)
    after_cross = (
        after_self
        + jnp.dot(heads_cross_low, weights[:, 7 * D :], preferred_element_type=single)
        + cross_output
    )
    normed_feed = layer_norm(after_cross, gain_feed, shift_feed).astype(bfloat)
    part_rows = normed_feed
    inner_act = (
        jnp.dot(
            part_rows,
            lax.all_gather(up_weight, "fsdp", axis=0, tiled=True),
            preferred_element_type=single,
        )
        + bias_up
    )
    active = gelu_exact(inner_act).astype(bfloat)
    branch = times_t(active, lax.all_gather(down_weight, "fsdp", axis=0, tiled=True))
    mixed = (after_cross + branch + bias_down).astype(bfloat)
    grad_top = cotangent[0]
    part_rows = grad_top
    grad_active = jnp.dot(
        part_rows,
        lax.all_gather(down_weight, "fsdp", axis=0, tiled=True),
        preferred_element_type=single,
    )
    _, gelu_pull = jax.vjp(gelu_exact, inner_act)
    grad_inner = gelu_pull(grad_active)[0].astype(bfloat)
    grad_normed_feed = times_t(grad_inner, lax.all_gather(up_weight, "fsdp", axis=0, tiled=True))
    back_feed, gain_feed_grad, shift_feed_grad = norm_back(
        after_cross, gain_feed, shift_feed, grad_normed_feed
    )
    grad_cross_in = grad_top.astype(single) + back_feed
    again = lax.all_gather(attn_weight, "fsdp", axis=0, tiled=True)
    grad_branch_cross = grad_cross_in.astype(bfloat)
    grad_heads_cross = times_t(grad_branch_cross, again[:, 7 * D :]).astype(bfloat)
    delta_cross = jnp.sum(
        (grad_heads_cross.astype(single) * heads_cross).reshape(row_count, H, HD), axis=-1
    )
    query_grad_cross, key_grad_cross, value_grad_cross = cycle_back(
        query_cross,
        grad_heads_cross,
        total_cross,
        delta_cross,
        query_seg,
        query_pos,
        False,
        key_cross,
        value_cross,
        source_seg,
    )
    query_grad_cross = query_grad_cross.astype(bfloat)
    kv_grad_cross = jnp.concatenate([key_grad_cross, value_grad_cross], axis=1).astype(bfloat)
    grad_encoder = times_t(kv_grad_cross, again[:, 5 * D : 7 * D])
    grad_normed_cross = times_t(query_grad_cross, again[:, 4 * D : 5 * D])
    back_cross, gain_cross_grad, shift_cross_grad = norm_back(
        after_self, gain_cross, shift_cross, grad_normed_cross
    )
    grad_self_in = grad_cross_in + back_cross
    grad_branch_self = grad_self_in.astype(bfloat)
    grad_heads_self = times_t(grad_branch_self, again[:, 3 * D : 4 * D]).astype(bfloat)
    delta_self = jnp.sum(
        (grad_heads_self.astype(single) * heads_self).reshape(row_count, H, HD), axis=-1
    )
    query_grad_self, key_grad_self, value_grad_self = cycle_back(
        query_self,
        grad_heads_self,
        total_self,
        delta_self,
        query_seg,
        query_pos,
        True,
        key_self,
        value_self,
        query_seg,
    )
    qkv_grad_self = jnp.concatenate(
        [query_grad_self, key_grad_self, value_grad_self], axis=1
    ).astype(bfloat)
    grad_normed_self = times_t(qkv_grad_self, again[:, : 3 * D])
    back_self, gain_self_grad, shift_self_grad = norm_back(
        stream, gain_self, shift_self, grad_normed_self
    )
    grad_tokens = grad_self_in + back_self

    def slab(left, right):
        return lax.dot_general(left, right, (((0,), (0,)), ((), ())), preferred_element_type=single)

    summed = lax.psum_scatter(
        jnp.concatenate(
            [
                slab(normed_self, qkv_grad_self),
                slab(heads_self_low, grad_branch_self),
                slab(normed_cross, query_grad_cross),
                slab(source, kv_grad_cross),
                slab(heads_cross_low, grad_branch_cross),
                slab(normed_feed, grad_inner),
                slab(grad_top, active),
            ],
            axis=1,
        ),
        ("ctx", "fsdp"),
        scatter_dimension=0,
        tiled=True,
    )
    vector_terms = jnp.concatenate(
        [
            jnp.stack(
                [
                    gain_self_grad,
                    shift_self_grad,
                    gain_cross_grad,
                    shift_cross_grad,
                    gain_feed_grad,
                    shift_feed_grad,
                    column_sum(qkv_grad_self[:, :D]),
                    column_sum(qkv_grad_self[:, 2 * D :]),
                    column_sum(grad_branch_self),
                    column_sum(query_grad_cross),
                    column_sum(kv_grad_cross[:, D:]),
                    column_sum(grad_branch_cross),
                    column_sum(grad_top),
                ]
            ),
            column_sum(grad_inner).reshape(-1, D),
        ],
        axis=0,
    )
    grad_vectors = lax.psum(vector_terms, ("ctx", "fsdp"))
    hidden_width = up_weight.shape[1]
    return (
        mixed[None],
        grad_tokens[None],
        grad_encoder[None],
        summed[:, : 8 * D],
        summed[:, 8 * D : 8 * D + hidden_width],
        summed[:, 8 * D + hidden_width :],
        grad_vectors,
    )


def solution(mesh):
    return jax.shard_map(
        body,
        mesh=mesh,
        in_specs=(
            P("fsdp", "ctx", None),
            P("fsdp", "ctx", None),
            P("fsdp", "ctx"),
            P("fsdp", "ctx"),
            P("fsdp", None),
            P("fsdp", None),
            P("fsdp", None),
            P(),
            P("fsdp", "ctx", None),
        ),
        out_specs=(
            P("fsdp", "ctx", None),
            P("fsdp", "ctx", None),
            P("fsdp", "ctx", None),
            P(("ctx", "fsdp"), None),
            P(("ctx", "fsdp"), None),
            P(("ctx", "fsdp"), None),
            P(),
        ),
        check_vma=False,
    )
```

profile of v0, /device:TPU:8, one launch (start us, length us, event | category | flops | bytes accessed | tf_op | source)
XLA Modules:
  0.0 2375.9 jit_solution(7303155084781232535)
XLA Ops:
  8.8 285.8 %all-gather.10.cloned.1.call-done = bf16[1024,8192]{1,0:T(8,128)(2,1)} async-done(((bf16[256,8192]{1,0:T(8,128)(2,1)}), bf16[1024,8192]{1,0:T(8,128)(2,1)}) %all-gather.10.cloned.1.call-update) | async-done | bytes 16777232 | tf_op jit(solution)/shard_map/all_gather | solution.py:217
  308.8 8.9 all-gather
  320.5 13.2 all-reduce.1
  340.9 8.3 all-gather.18.cloned.1.call-done
  351.4 28.0 %all-gather.12.cloned.1.call-done = bf16[1024,1024]{1,0:T(8,128)(2,1)} async-done(((bf16[128,1024]{1,0:T(8,128)(2,1)}), bf16[1024,1024]{1,0:T(8,128)(2,1)}) %all-gather.12.cloned.1.call-update) | async-done | bytes 2097168 | tf_op jit(solution)/shard_map/all_gather | solution.py:239
  383.4 26.3 %all-gather.14.cloned.1.call-done = bf16[1024,1024]{1,0:T(8,128)(2,1)} async-done(((bf16[128,1024]{1,0:T(8,128)(2,1)}), bf16[1024,1024]{1,0:T(8,128)(2,1)}) %all-gather.14.cloned.1.call-update) | async-done | bytes 2097168 | tf_op jit(solution)/shard_map/all_gather | solution.py:238
  434.0 260.9 %all-gather.20.cloned.1.call-done = bf16[1024,8192]{1,0:T(8,128)(2,1)} async-done(((bf16[256,8192]{1,0:T(8,128)(2,1)}), bf16[1024,8192]{1,0:T(8,128)(2,1)}) %all-gather.20.cloned.1.call-update) | async-done | bytes 16777232 | tf_op jit(solution)/shard_map/all_gather | solution.py:289
  694.9 10.2 convolution_add_fusion
  705.1 276.4 %all-gather.22.cloned.1.call-done = bf16[1024,8192]{1,0:T(8,128)(2,1)} async-done(((bf16[256,8192]{1,0:T(8,128)(2,1)}), bf16[1024,8192]{1,0:T(8,128)(2,1)}) %all-gather.22.cloned.1.call-update) | async-done | bytes 16777232 | tf_op jit(solution)/shard_map/all_gather | solution.py:295
  981.5 17.1 convert_reduce_fusion
  998.6 13.5 multiply_reduce_fusion
  1019.7 151.5 %while.47 = (s32[]{:T(128)}, f32[128,1024]{0,1:T(8,128)S(1)}, bf16[64,1024]{0,1:T(8,128)(2,1)}, bf16[64,1024]{1,0:T(8,128)(2,1)}, bf16[64]{0:T(256)(128)(2,1)}, ...) while((s32[]{:T(128)}, f32[128,1024]{0,1:T(8,128)S(1)}, ...), condition=%wide.region_14.15_spmd.clone, body=%wide.region_13.14_spmd.clone.sunk | while | flops 85729280 | bytes 13534681 | solution.py:173
  1182.0 162.9 %while.48 = (s32[]{:T(128)}, f32[128,1024]{0,1:T(8,128)S(1)}, bf16[128,1024]{0,1:T(8,128)(2,1)}, bf16[128,1024]{0,1:T(8,128)(2,1)}, bf16[128]{0:T(256)(128)(2,1)...) while((s32[]{:T(128)}, f32[128,1024]{0,1:T(8,128)S(1)}, ...), condition=%wide.region_19.20_spmd.clone, body=%wide.region_18.19_spmd.clone.sunk | while | flops 171262224 | bytes 19190284 | solution.py:173
  1347.8 7.5 convolution_dynamic-update-slice_fusion.1
  1360.9 4.5 convolution_bitcast_fusion.4
  1365.4 9.2 copy.72
  1374.6 7.8 constant_dynamic-update-slice_fusion
  1385.0 13.3 convolution_dynamic-update-slice_fusion
  1398.4 15.0 bitcast_dynamic-update-slice_fusion
  1414.5 5.1 fusion.163
  1423.9 5.4 fusion.108
  1429.3 16.6 fusion.111
  1445.9 792.8 %reduce-scatter.2.cloned.1.call-done = f32[32,24576]{1,0:T(8,128)} async-done(((f32[1024,24576]{1,0:T(8,128)}), f32[32,24576]{1,0:T(8,128)}) %reduce-scatter.2.cloned.1.call-update) | async-done | bytes 3145744 | tf_op jit(solution)/shard_map/reduce_scatter | solution.py:366
  2242.3 125.4 %all-reduce.4.cloned.1.call-done = f32[21,1024]{1,0:T(8,128)} async-done(((f32[21,1024]{1,0:T(8,128)}), f32[21,1024]{1,0:T(8,128)}) %all-reduce.4.cloned.1.call-update) | async-done | bytes 86032 | tf_op jit(solution)/shard_map/psum | solution.py:406
  (720 shorter events, 406.8 us)
Async XLA Ops:
  7.2 287.4 %all-gather.10.cloned.1.call-start = ((), (), s32[]{:S(2)}) async-start(), calls=%async_computation.1 | async-start | bytes 20971520 | tf_op jit(solution)/shard_map/all_gather | solution.py:217
  7.9 330.6 %all-gather.16.cloned.1.call-start = ((), (), s32[]{:S(2)}) async-start(), calls=%async_computation.4 | async-start | bytes 1179648 | tf_op jit(solution)/shard_map/all_gather | solution.py:271
  298.4 50.8 %all-gather.18.cloned.1.call-start = ((), (), s32[]{:S(2)}) async-start(), calls=%async_computation.5 | async-start | bytes 1179648 | tf_op jit(solution)/shard_map/all_gather | solution.py:270
  299.1 80.3 %all-gather.12.cloned.1.call-start = ((), (), s32[]{:S(2)}) async-start(), calls=%async_computation.2 | async-start | bytes 2359296 | tf_op jit(solution)/shard_map/all_gather | solution.py:239
  304.4 105.3 %all-gather.14.cloned.1.call-start = ((), (), s32[]{:S(2)}) async-start(), calls=%async_computation.3 | async-start | bytes 2359296 | tf_op jit(solution)/shard_map/all_gather | solution.py:238
  305.0 389.9 %all-gather.20.cloned.1.call-start = ((), (), s32[]{:S(2)}) async-start(), calls=%async_computation.6 | async-start | bytes 20971520 | tf_op jit(solution)/shard_map/all_gather | solution.py:289
  305.6 675.9 %all-gather.22.cloned.1.call-start = ((), (), s32[]{:S(2)}) async-start(), calls=%async_computation.7 | async-start | bytes 20971520 | tf_op jit(solution)/shard_map/all_gather | solution.py:295
  306.4 1932.4 %reduce-scatter.2.cloned.1.call-start = ((), (), s32[]{:S(2)}) async-start(), calls=%async_computation.8 | async-start | bytes 103809024 | tf_op jit(solution)/shard_map/reduce_scatter | solution.py:366
  1057.4 18.7 collective-permute-start
  1095.6 18.7 collective-permute-start
  1133.9 18.7 collective-permute-start
  1183.0 19.9 collective-permute-start.5
  1183.9 18.9 collective-permute-start.6
  1203.8 18.9 collective-permute-start.5
  1223.7 19.7 collective-permute-start.5
  1224.6 18.8 collective-permute-start.6
  1244.4 18.9 collective-permute-start.5
  1264.3 19.7 collective-permute-start.5
  1265.2 18.8 collective-permute-start.6
  1285.0 18.9 collective-permute-start.5
  1304.9 19.7 collective-permute-start.5
  1305.8 18.8 collective-permute-start.6
  1325.6 18.9 collective-permute-start.5
  1413.4 954.3 %all-reduce.4.cloned.1.call-start = ((), (), s32[]{:S(2)}) async-start(), calls=%async_computation.9 | async-start | bytes 196608 | tf_op jit(solution)/shard_map/psum | solution.py:406
  (149 other events, 4740.2 us)
Sparse Core Ops, SparseCore 0:
  9.6 284.9 all-gather.9
  298.5 24.6 all-gather.15
  325.7 23.4 all-gather.17
  351.5 27.8 all-gather.11
  381.7 27.8 all-gather.13
  411.1 283.7 all-gather.19
  696.5 284.9 all-gather.21
  1413.5 825.1 reduce-scatter.1
  2244.9 122.7 all-reduce.3
where the time goes:
time: 2390 us; the launch traced here: 2380 us
  waiting for transfers between devices  1890 us (79%)
  matrix products  192 us (8%)
  local copies, waits for them, and re-layouts  121 us (5%)
  other arithmetic  90.9 us (4%)
  starting transfers between devices  45 us (2%)
    reduce_scatter x1, waiting for transfers between devices, body(): lax.psum_scatter(jnp.concatenate([slab(normed_self, qkv_grad_self), slab(...  793 us
    all_gather x1, waiting for transfers between devices, body(): weights = lax.all_gather(attn_weight, 'fsdp', axis=0, tiled=True)  286 us
    all_gather x1, waiting for transfers between devices, body(): lax.all_gather(down_weight, 'fsdp', axis=0, tiled=True)  276 us
    all_gather x1, waiting for transfers between devices, body(): lax.all_gather(up_weight, 'fsdp', axis=0, tiled=True)  261 us
    psum x1, waiting for transfers between devices, body(): grad_vectors = lax.psum(vector_terms, ('ctx', 'fsdp'))  125 us
    ppermute x80, waiting for transfers between devices, passed_along(): lax.ppermute(array, axis, [(i, (i + by) % size) for i in range(size)])  79.3 us
    while x48, local copies, waits for them, and re-layouts  54.4 us
    dot_general x7, matrix products, times_t(): lax.dot_general(left, right, (((1,), (1,)), ((), ())), preferred_element_...  50.1 us
  transfers between devices with their start and end apart: 89, of which 37 were waited for; matrix products, arithmetic and copies ran while one was open for 11% of the time, Pallas kernels for 0%

commit v1 on v0

v1 whole, which is shorter than its diff:
```python
import jax
import jax.numpy as jnp
from jax import lax
from jax.sharding import PartitionSpec as P

D = 1024
H = 16
HD = 64
EPS = 1e-05
NEG = -1e30
SCALE = HD ** (-0.5)
bf = jnp.bfloat16
f32 = jnp.float32


def layer_norm(value, gain, shift):
    mean_row = jnp.mean(value, axis=-1, keepdims=True)
    centred = value - mean_row
    spread = jnp.mean(centred * centred, axis=-1, keepdims=True)
    return centred * lax.rsqrt(spread + EPS) * gain + shift


def norm_back(value, gain, grad):
    mean_row = jnp.mean(value, axis=-1, keepdims=True)
    centred = value - mean_row
    inv = lax.rsqrt(jnp.mean(centred * centred, axis=-1, keepdims=True) + EPS)
    hat = centred * inv
    gg = grad * gain
    back = inv * (gg - jnp.mean(gg, axis=-1, keepdims=True) - hat * jnp.mean(gg * hat, axis=-1, keepdims=True))
    return back, jnp.sum(grad * hat, axis=0), jnp.sum(grad, axis=0)


def dot(a, b):
    return jnp.dot(a, b, preferred_element_type=f32)


def dot_t(a, b):
    return lax.dot_general(a, b, (((1,), (1,)), ((), ())), preferred_element_type=f32)


def t_dot(a, b):
    return lax.dot_general(a, b, (((0,), (0,)), ((), ())), preferred_element_type=f32)


def gather(a):
    return lax.all_gather(a, "ctx", axis=0, tiled=True)


def scatter(a):
    return lax.psum_scatter(a.astype(bf), "ctx", scatter_dimension=0, tiled=True).astype(f32)


def heads(a):
    return a.reshape(a.shape[0], -1, HD)


def attend(q, k, v, allowed):
    s = jnp.einsum("qhd,khd->hqk", heads(q), heads(k), preferred_element_type=f32) * SCALE
    s = jnp.where(allowed[None], s, NEG)
    m = jnp.max(s, axis=-1, keepdims=True)
    e = jnp.exp(s - m)
    tot = jnp.sum(e, axis=-1, keepdims=True)
    p = (e / tot).astype(bf)
    o = jnp.einsum("hqk,khd->qhd", p, heads(v), preferred_element_type=f32).reshape(q.shape)
    return o, m + jnp.log(tot)


def attend_back(q, k, v, allowed, o, lse, do):
    s = jnp.einsum("qhd,khd->hqk", heads(q), heads(k), preferred_element_type=f32) * SCALE
    p = jnp.where(allowed[None], jnp.exp(s - lse), 0.0)
    delta = jnp.sum(heads(do.astype(f32) * o), axis=-1).T[..., None]
    dv = jnp.einsum("hqk,qhd->khd", p.astype(bf), heads(do), preferred_element_type=f32).reshape(k.shape)
    dp = jnp.einsum("qhd,khd->hqk", heads(do), heads(v), preferred_element_type=f32)
    ds = (p * (dp - delta) * SCALE).astype(bf)
    dq = jnp.einsum("hqk,khd->qhd", ds, heads(k), preferred_element_type=f32).reshape(q.shape)
    dk = jnp.einsum("hqk,qhd->khd", ds, heads(q), preferred_element_type=f32).reshape(k.shape)
    return dq.astype(bf), dk.astype(bf), dv.astype(bf)


def columns(a, width):
    return lax.dynamic_slice_in_dim(a, lax.axis_index("ctx") * width, width, axis=a.ndim - 1)


def body(tokens, encoder, dec_seg, src_seg, attn_w, up_w, down_w, vec, cot):
    n = lax.axis_size("ctx")
    nz = lax.axis_size("fsdp")
    w = D // n
    ff = up_w.shape[1]
    fw = ff // n
    x = tokens[0].astype(f32)
    t = x.shape[0]
    length = n * t
    g = cot[0]
    g1, s1, g2, s2, g3, s3, bq, bv, bo, bqc, bvc, boc, bdown = [vec[i] for i in range(13)]
    bup = columns(vec[13:].reshape(-1), fw)
    rows = attn_w.shape[0]
    mine = columns(attn_w.reshape(rows, 8, D), w).reshape(rows, 8 * w)
    wa = lax.all_gather(mine, "fsdp", axis=0, tiled=True).reshape(D, 8, w)
    up = lax.all_gather(columns(up_w, fw), "fsdp", axis=0, tiled=True)
    down = lax.all_gather(columns(down_w, fw), "fsdp", axis=0, tiled=True)
    wqkv = jnp.concatenate([wa[:, 0], wa[:, 1], wa[:, 2]], axis=1)
    wkvc = jnp.concatenate([wa[:, 5], wa[:, 6]], axis=1)
    outs = jnp.concatenate([wa[:, 3], wa[:, 7]], axis=1)
    outs = lax.all_to_all(outs.reshape(n, w, 2 * w), "ctx", 0, 0, tiled=False)
    outs = jnp.transpose(outs.reshape(n, w, 2, w), (2, 1, 0, 3)).reshape(2, w, D)
    wo, woc = outs[0], outs[1]

    seg = gather(dec_seg[0])
    src = gather(src_seg[0])
    pos = jnp.arange(length)
    causal = (seg[:, None] == seg[None, :]) & (pos[:, None] >= pos[None, :])
    crossed = seg[:, None] == src[None, :]
    gf = gather(g)
    ef = gather(encoder[0])

    n1f = gather(layer_norm(x, g1, s1).astype(bf))
    zero = jnp.zeros((w,), f32)
    qkv = (dot(n1f, wqkv) + jnp.concatenate([columns(bq, w), zero, columns(bv, w)])).astype(bf)
    q1, k1, v1 = qkv[:, :w], qkv[:, w:2 * w], qkv[:, 2 * w:]
    o1, lse1 = attend(q1, k1, v1, causal)
    o1b = o1.astype(bf)
    x1 = x + scatter(dot(o1b, wo)) + bo
    n2f = gather(layer_norm(x1, g2, s2).astype(bf))
    q2 = (dot(n2f, wa[:, 4]) + columns(bqc, w)).astype(bf)
    kv2 = (dot(ef, wkvc) + jnp.concatenate([zero, columns(bvc, w)])).astype(bf)
    k2, v2 = kv2[:, :w], kv2[:, w:]
    o2, lse2 = attend(q2, k2, v2, crossed)
    o2b = o2.astype(bf)
    x2 = x1 + scatter(dot(o2b, woc)) + boc
    n3f = gather(layer_norm(x2, g3, s3).astype(bf))
    u = dot(n3f, up) + bup
    cdf = 0.5 * (1.0 + lax.erf(u * (2.0 ** -0.5)))
    act = (u * cdf).astype(bf)
    mixed = (x2 + scatter(dot_t(act, down)) + bdown).astype(bf)
    da = dot(gf, down)
    slope = cdf + u * jnp.exp(-0.5 * u * u) * ((2.0 * jnp.pi) ** -0.5)
    du = (da * slope).astype(bf)
    back3, gg3, gs3 = norm_back(x2, g3, scatter(dot_t(du, up)))
    dx2 = g.astype(f32) + back3
    dy2 = dx2.astype(bf)
    dy2f = gather(dy2)
    do2 = dot_t(dy2f, woc).astype(bf)
    dq2, dk2, dv2 = attend_back(q2, k2, v2, crossed, o2, lse2, do2)
    dkv2 = jnp.concatenate([dk2, dv2], axis=1)
    grad_encoder = scatter(dot_t(dkv2, wkvc))
    back2, gg2, gs2 = norm_back(x1, g2, scatter(dot_t(dq2, wa[:, 4])))
    dx1 = dx2 + back2
    dy1 = dx1.astype(bf)
    dy1f = gather(dy1)
    do1 = dot_t(dy1f, wo).astype(bf)
    dq1, dk1, dv1 = attend_back(q1, k1, v1, causal, o1, lse1, do1)
    dqkv = jnp.concatenate([dq1, dk1, dv1], axis=1)
    back1, gg1, gs1 = norm_back(x, g1, scatter(dot_t(dqkv, wqkv)))
    grad_tokens = dx1 + back1

    def owned(part):
        m = part.shape[1]
        share = D // (n * nz)
        part = part.astype(bf).reshape(n, nz, share, m)
        part = jnp.transpose(part, (1, 0, 2, 3))
        summed = lax.psum_scatter(part, "fsdp", scatter_dimension=0, tiled=False)
        got = lax.all_to_all(summed, "ctx", 0, 0, tiled=False)
        return got.astype(f32)

    share = D // (n * nz)
    grad_o1 = t_dot(o1b, dy1f)
    grad_o2 = t_dot(o2b, dy2f)
    both = jnp.concatenate([grad_o1, grad_o2], axis=1).astype(bf)
    both = lax.psum_scatter(both, "fsdp", scatter_dimension=0, tiled=True).astype(f32)
    part = jnp.concatenate([t_dot(n1f, dqkv), t_dot(n2f, dq2), t_dot(ef, dkv2)], axis=1)
    part = owned(part).reshape(n, share, 6, w)
    part = jnp.transpose(part, (1, 2, 0, 3)).reshape(share, 6, D)
    grad_attn = jnp.concatenate(
        [part[:, 0], part[:, 1], part[:, 2], both[:, :D], part[:, 3], part[:, 4], part[:, 5], both[:, D:]], axis=1)
    grad_up = jnp.transpose(owned(t_dot(n3f, du)), (1, 0, 2)).reshape(share, ff)
    grad_down = jnp.transpose(owned(t_dot(gf, act)), (1, 0, 2)).reshape(share, ff)

    def csum(a):
        return jnp.sum(a.astype(f32), axis=0)

    def place(vals, total):
        return lax.dynamic_update_slice(jnp.zeros((total,), f32), vals, (lax.axis_index("ctx") * vals.shape[0],))

    terms = jnp.concatenate([
        jnp.stack([gg1, gs1, gg2, gs2, gg3, gs3, place(csum(dq1), D), place(csum(dv1), D), csum(dy1), place(csum(dq2), D),
                   place(csum(dv2), D), csum(dy2), csum(g)]),
        place(csum(du), ff).reshape(-1, D)], axis=0)
    grad_vectors = lax.psum(terms, ("ctx", "fsdp"))
    return (mixed[None], grad_tokens[None], grad_encoder[None], grad_attn, grad_up, grad_down, grad_vectors)


def solution(mesh):
    return jax.shard_map(
        body, mesh=mesh,
        in_specs=(P("fsdp", "ctx", None), P("fsdp", "ctx", None), P("fsdp", "ctx"), P("fsdp", "ctx"), P("fsdp", None),
                  P("fsdp", None), P("fsdp", None), P(), P("fsdp", "ctx", None)),
        out_specs=(P("fsdp", "ctx", None), P("fsdp", "ctx", None), P("fsdp", "ctx", None), P(("ctx", "fsdp"), None),
                   P(("ctx", "fsdp"), None), P(("ctx", "fsdp"), None), P()),
        check_vma=False,
    )
```

time: 2390 us -> 1070 us (0.45)
  waiting for transfers between devices: 1890 us -> 831 us
  matrix products: 192 us -> 101 us
  local copies, waits for them, and re-layouts: 121 us -> 42.6 us
  other arithmetic: 90.9 us -> 32.7 us
  starting transfers between devices: 45 us -> 16 us
    all_gather x7 -> x10, waiting for transfers between devices: 886 us -> 271 us  [the longest x7 147 us: gather(): return lax.all_gather(a, 'ctx', axis=0, tiled=True)]
    reduce_scatter x1 -> x9, waiting for transfers between devices: 793 us -> 305 us  [the longest x7 254 us: scatter(): lax.psum_scatter(a.astype(bf), 'ctx', scatter_dimension=0, tiled=True)]
    unnamed x9 -> x22, waiting for transfers between devices: 3.18 us -> 116 us
    dot_general x105 -> x33, matrix products: 192 us -> 101 us  [the longest x7 25.4 us: dot(): return jnp.dot(a, b, preferred_element_type=f32)]
    ppermute x80 -> x0, waiting for transfers between devices: 79.3 us -> none  [passed_along(): lax.ppermute(array, axis, [(i, (i + by) % size) for i in range(size)])]
    while x48 -> x0, local copies, waits for them, and re-layouts: 54.4 us -> none
    convert_element_type x65 -> x6, other arithmetic: 54.1 us -> 6.05 us  [the longest x1 1.82 us: body(): n2f = gather(layer_norm(x1, g2, s2).astype(bf))]
    ppermute x80 -> x0, starting transfers between devices: 44.4 us -> none  [passed_along(): lax.ppermute(array, axis, [(i, (i + by) % size) for i in range(size)])]
  transfers between devices with their start and end apart: 89 -> 25, of which waited for: 37 -> 24; matrix products, arithmetic and copies ran while one was open for 11% -> 10% of each run, Pallas kernels for 0% -> 0%
where the time goes in v1:
time: 1070 us; the launch traced here: 1060 us
  waiting for transfers between devices  831 us (78%)
  matrix products  101 us (9%)
  local copies, waits for them, and re-layouts  42.6 us (4%)
  other arithmetic  32.7 us (3%)
  blocking collectives  22.6 us (2%)
  between operations  16.6 us (2%)
  starting transfers between devices  16 us (1%)
    reduce_scatter x7, waiting for transfers between devices, scatter(): lax.psum_scatter(a.astype(bf), 'ctx', scatter_dimension=0, tiled=True)  254 us
    all_gather x7, waiting for transfers between devices, gather(): return lax.all_gather(a, 'ctx', axis=0, tiled=True)  147 us
    psum x1, waiting for transfers between devices, body(): grad_vectors = lax.psum(terms, ('ctx', 'fsdp'))  116 us
    unnamed x22, waiting for transfers between devices  116 us
    all_gather x1, waiting for transfers between devices, body(): wa = lax.all_gather(mine, 'fsdp', axis=0, tiled=True).reshape(D, 8, w)  44.2 us
    all_gather x1, waiting for transfers between devices, body(): up = lax.all_gather(columns(up_w, fw), 'fsdp', axis=0, tiled=True)  40.7 us
    all_gather x1, waiting for transfers between devices, body(): down = lax.all_gather(columns(down_w, fw), 'fsdp', axis=0, tiled=True)  39.1 us
    reduce_scatter x1, waiting for transfers between devices, owned(): summed = lax.psum_scatter(part, 'fsdp', scatter_dimension=0, tiled=False)  32.4 us
  transfers between devices with their start and end apart: 25, of which 24 were waited for; matrix products, arithmetic and copies ran while one was open for 10% of the time, Pallas kernels for 0%

profile of v1, /device:TPU:8, one launch (start us, length us, event | category | flops | bytes accessed | tf_op | source)
XLA Modules:
  0.0 1062.8 jit_solution(18306361702792189424)
XLA Ops:
  17.6 44.2 %all-gather.17.cloned.1.call-done = bf16[1024,1024]{0,1:T(8,128)(2,1)} async-done(((bf16[256,1024]{0,1:T(8,128)(2,1)}), bf16[1024,1024]{0,1:T(8,128)(2,1)}) %all-gather.17.cloned.1.call-update) | async-done | bytes 2097168 | tf_op jit(solution)/shard_map/all_gather | solution.py:98
  69.0 14.9 %all-gather = s32[1,1024]{1,0:T(1,128)S(1)} all-gather(s32[1,128]{1,0:T(1,128)S(1)} %copy-done.58), channel_id=2, replica_groups=mesh['ctx'=8,'fsdp'=4] {'ctx'}, dimensions={1}, use_global_device_ids=true | all-gather | bytes 4608 | tf_op jit(solution)/shard_map/all_gather | solution.py:46
  85.2 9.0 all-gather.15.cloned.1.call-done
  109.1 40.7 %reduce-scatter.16.cloned.1.call-done = bf16[128,1024]{1,0:T(8,128)(2,1)} async-done(((bf16[1024,1024]{1,0:T(8,128)(2,1)}), bf16[128,1024]{1,0:T(8,128)(2,1)}) %reduce-scatter.16.cloned.1.call-update) | async-done | bytes 262160 | tf_op jit(solution)/shard_map/reduce_scatter | solution.py:50
  155.4 7.7 all-reduce.1
  163.5 11.8 %all-gather.31.cloned.1.call-done = bf16[1,512,1024]{2,1,0:T(8,128)(2,1)} async-done(((bf16[1,64,1024]{2,1,0:T(8,128)(2,1)}), bf16[1,512,1024]{2,1,0:T(8,128)(2,1)}) %all-gather.31.cloned.1.call-update) | async-done | bytes 1048592 | tf_op jit(solution)/shard_map/all_gather | solution.py:46
  177.0 28.7 %all-gather.19.cloned.1.call-done = bf16[1024,1024]{1,0:T(8,128)(2,1)} async-done(((bf16[128,1024]{1,0:T(8,128)(2,1)}), bf16[1024,1024]{1,0:T(8,128)(2,1)}) %all-gather.19.cloned.1.call-update) | async-done | bytes 2097168 | tf_op jit(solution)/shard_map/all_gather | solution.py:46
  216.5 39.4 %reduce-scatter.18.cloned.1.call-done = bf16[128,1024]{1,0:T(8,128)(2,1)} async-done(((bf16[1024,1024]{1,0:T(8,128)(2,1)}), bf16[128,1024]{1,0:T(8,128)(2,1)}) %reduce-scatter.18.cloned.1.call-update) | async-done | bytes 262160 | tf_op jit(solution)/shard_map/reduce_scatter | solution.py:50
  261.7 40.7 %all-gather.23.cloned.1.call-done = bf16[1024,1024]{1,0:T(8,128)(2,1)} async-done(((bf16[256,1024]{1,0:T(8,128)(2,1)}), bf16[1024,1024]{1,0:T(8,128)(2,1)}) %all-gather.23.cloned.1.call-update) | async-done | bytes 2097168 | tf_op jit(solution)/shard_map/all_gather | solution.py:99
  302.4 30.7 %all-gather.21.cloned.1.call-done = bf16[1024,1024]{1,0:T(8,128)(2,1)} async-done(((bf16[128,1024]{1,0:T(8,128)(2,1)}), bf16[1024,1024]{1,0:T(8,128)(2,1)}) %all-gather.21.cloned.1.call-update) | async-done | bytes 2097168 | tf_op jit(solution)/shard_map/all_gather | solution.py:46
  340.5 39.1 %all-gather.25.cloned.1.call-done = bf16[1024,1024]{1,0:T(8,128)(2,1)} async-done(((bf16[256,1024]{1,0:T(8,128)(2,1)}), bf16[1024,1024]{1,0:T(8,128)(2,1)}) %all-gather.25.cloned.1.call-update) | async-done | bytes 2097168 | tf_op jit(solution)/shard_map/all_gather | solution.py:100
  379.6 30.0 %all-gather.33.cloned.1.call-done = bf16[1,1024,1024]{2,1,0:T(8,128)(2,1)} async-done(((bf16[1,128,1024]{2,1,0:T(8,128)(2,1)}), bf16[1,1024,1024]{2,1,0:T(8,128)(2,1)}) %all-gather.33.cloned.1.call-update) | async-done | bytes 2097168 | tf_op jit(solution)/shard_map/all_gather | solution.py:46
  428.1 35.1 %reduce-scatter.22.cloned.1.call-done = bf16[128,1024]{1,0:T(8,128)(2,1)} async-done(((bf16[1024,1024]{1,0:T(8,128)(2,1)}), bf16[128,1024]{1,0:T(8,128)(2,1)}) %reduce-scatter.22.cloned.1.call-update) | async-done | bytes 262160 | tf_op jit(solution)/shard_map/reduce_scatter | solution.py:50
  465.0 42.9 %reduce-scatter.20.cloned.1.call-done = bf16[128,1024]{1,0:T(8,128)(2,1)} async-done(((bf16[1024,1024]{1,0:T(8,128)(2,1)}), bf16[128,1024]{1,0:T(8,128)(2,1)}) %reduce-scatter.20.cloned.1.call-update) | async-done | bytes 262160 | tf_op jit(solution)/shard_map/reduce_scatter | solution.py:50
  510.9 28.0 %all-gather.27.cloned.1.call-done = bf16[1024,1024]{1,0:T(8,128)(2,1)} async-done(((bf16[128,1024]{1,0:T(8,128)(2,1)}), bf16[1024,1024]{1,0:T(8,128)(2,1)}) %all-gather.27.cloned.1.call-update) | async-done | bytes 2097168 | tf_op jit(solution)/shard_map/all_gather | solution.py:46
  550.1 41.3 %reduce-scatter.24.cloned.1.call-done = bf16[128,1024]{1,0:T(8,128)(2,1)} async-done(((bf16[1024,1024]{1,0:T(8,128)(2,1)}), bf16[128,1024]{1,0:T(8,128)(2,1)}) %reduce-scatter.24.cloned.1.call-update) | async-done | bytes 262160 | tf_op jit(solution)/shard_map/reduce_scatter | solution.py:50
  615.1 8.5 all-gather.29.cloned.1.call-done
  664.9 114.4 %all-reduce.10.cloned.1.call-done = (bf16[4,8,32,1024]{3,2,0,1:T(8,128)(2,1)}, bf16[4,8,32,1024]{3,2,0,1:T(8,128)(2,1)}) async-done(((bf16[4,8,32,1024]{3,2,0,1:T(8,128)(2,1)}, bf16[4,8,32,1024]{3,2,0,1:T(8,128)(2,1)}), (bf16[4,8,32,1024]{3,2,0,1:T(8,128)(2,1)}, bf16[4,8,32,1024]{3,2,0,1:T(8,128)(2,1)})) %all-reduce.10.cloned.1.call-update) | async-done | bytes 4194320
  800.6 9.6 all-to-all-done.3
  811.7 9.8 reduce-scatter.28.cloned.1.call-done
  823.3 18.9 %reduce-scatter.32.cloned.1.call-done = bf16[32,2048]{1,0:T(8,128)(2,1)} async-done(((bf16[128,2048]{1,0:T(8,128)(2,1)}), bf16[32,2048]{1,0:T(8,128)(2,1)}) %reduce-scatter.32.cloned.1.call-update) | async-done | bytes 131088 | tf_op jit(solution)/shard_map/reduce_scatter | solution.py:169
  843.1 44.9 %reduce-scatter.26.cloned.1.call-done = bf16[128,1024]{1,0:T(8,128)(2,1)} async-done(((bf16[1024,1024]{1,0:T(8,128)(2,1)}), bf16[128,1024]{1,0:T(8,128)(2,1)}) %reduce-scatter.26.cloned.1.call-update) | async-done | bytes 262160 | tf_op jit(solution)/shard_map/reduce_scatter | solution.py:50
  892.1 32.4 %reduce-scatter.30.cloned.1.call-done = bf16[1,8,32,768]{3,2,1,0:T(8,128)(2,1)} async-done(((bf16[4,8,32,768]{3,2,1,0:T(8,128)(2,1)}), bf16[1,8,32,768]{3,2,1,0:T(8,128)(2,1)}) %reduce-scatter.30.cloned.1.call-update) | async-done | bytes 393232 | tf_op jit(solution)/shard_map/reduce_scatter | solution.py:161
  937.7 116.3 %all-reduce.8.cloned.1.call-done = f32[21,1024]{1,0:T(8,128)} async-done(((f32[21,1024]{1,0:T(8,128)}), f32[21,1024]{1,0:T(8,128)}) %all-reduce.8.cloned.1.call-update) | async-done | bytes 86032 | tf_op jit(solution)/shard_map/psum | solution.py:188
  (323 shorter events, 207.3 us)
Async XLA Ops:
  7.2 54.6 %all-gather.17.cloned.1.call-start = ((), (), s32[]{:S(2)}) async-start(), calls=%async_computation.14 | async-start | bytes 2621440 | tf_op jit(solution)/shard_map/all_gather | solution.py:98
  15.6 78.7 %all-gather.15.cloned.1.call-start = ((), (), s32[]{:S(2)}) async-start(), calls=%async_computation.13 | async-start | bytes 2359296 | tf_op jit(solution)/shard_map/all_gather | solution.py:46
  65.4 19.1 %all-to-all-start = ((bf16[8,128,256]{2,1,0:T(8,128)(2,1)}), bf16[8,128,256]{2,1,0:T(8,128)(2,1)S(1)}, u32[]{:S(2)}, u32[]{:S(2)}) async-start(bf16[8,128,256]{2,1,0:T(8,128)(2,1)} %pad_maximum_fusion.3), calls=%async_computation | async-start | bytes 1048576 | tf_op jit(solution)/shard_map/all_to_all | solution.py:104
  68.9 80.9 %reduce-scatter.16.cloned.1.call-start = ((), (), s32[]{:S(2)}) async-start(), calls=%async_computation.15 | async-start | bytes 2359296 | tf_op jit(solution)/shard_map/reduce_scatter | solution.py:50
  108.5 66.8 %all-gather.31.cloned.1.call-start = ((), (), s32[]{:S(2)}) async-start(), calls=%async_computation.31 | async-start | bytes 1179648 | tf_op jit(solution)/shard_map/all_gather | solution.py:46
  109.0 96.6 %all-gather.19.cloned.1.call-start = ((), (), s32[]{:S(2)}) async-start(), calls=%async_computation.16 | async-start | bytes 2359296 | tf_op jit(solution)/shard_map/all_gather | solution.py:46
  154.0 102.0 %reduce-scatter.18.cloned.1.call-start = ((), (), s32[]{:S(2)}) async-start(), calls=%async_computation.17 | async-start | bytes 2359296 | tf_op jit(solution)/shard_map/reduce_scatter | solution.py:50
  214.5 87.9 %all-gather.23.cloned.1.call-start = ((), (), s32[]{:S(2)}) async-start(), calls=%async_computation.19 | async-start | bytes 2621440 | tf_op jit(solution)/shard_map/all_gather | solution.py:99
  216.5 116.6 %all-gather.21.cloned.1.call-start = ((), (), s32[]{:S(2)}) async-start(), calls=%async_computation.18 | async-start | bytes 2359296 | tf_op jit(solution)/shard_map/all_gather | solution.py:46
  258.2 121.4 %all-gather.25.cloned.1.call-start = ((), (), s32[]{:S(2)}) async-start(), calls=%async_computation.20 | async-start | bytes 2621440 | tf_op jit(solution)/shard_map/all_gather | solution.py:100
  260.2 149.5 %all-gather.33.cloned.1.call-start = ((), (), s32[]{:S(2)}) async-start(), calls=%async_computation.32 | async-start | bytes 2359296 | tf_op jit(solution)/shard_map/all_gather | solution.py:46
  260.8 202.4 %reduce-scatter.22.cloned.1.call-start = ((), (), s32[]{:S(2)}) async-start(), calls=%async_computation.22 | async-start | bytes 2359296 | tf_op jit(solution)/shard_map/reduce_scatter | solution.py:50
  421.8 86.1 %reduce-scatter.20.cloned.1.call-start = ((), (), s32[]{:S(2)}) async-start(), calls=%async_computation.21 | async-start | bytes 2359296 | tf_op jit(solution)/shard_map/reduce_scatter | solution.py:50
  428.0 110.8 %all-gather.27.cloned.1.call-start = ((), (), s32[]{:S(2)}) async-start(), calls=%async_computation.23 | async-start | bytes 2359296 | tf_op jit(solution)/shard_map/all_gather | solution.py:46
  510.8 80.6 %reduce-scatter.24.cloned.1.call-start = ((), (), s32[]{:S(2)}) async-start(), calls=%async_computation.24 | async-start | bytes 2359296 | tf_op jit(solution)/shard_map/reduce_scatter | solution.py:50
  550.0 73.6 %all-gather.29.cloned.1.call-start = ((), (), s32[]{:S(2)}) async-start(), calls=%async_computation.25 | async-start | bytes 2359296 | tf_op jit(solution)/shard_map/all_gather | solution.py:46
  595.6 183.7 %all-reduce.10.cloned.1.call-start = ((), (), s32[]{:S(2)}) async-start(), calls=%async_computation.33 | async-start | bytes 8388608
  605.6 215.8 %reduce-scatter.28.cloned.1.call-start = ((), (), s32[]{:S(2)}) async-start(), calls=%async_computation.27 | async-start | bytes 1179648 | tf_op jit(solution)/shard_map/reduce_scatter | solution.py:50
  612.9 229.3 %reduce-scatter.32.cloned.1.call-start = ((), (), s32[]{:S(2)}) async-start(), calls=%async_computation.29 | async-start | bytes 655360 | tf_op jit(solution)/shard_map/reduce_scatter | solution.py:169
  639.4 248.6 %reduce-scatter.26.cloned.1.call-start = ((), (), s32[]{:S(2)}) async-start(), calls=%async_computation.26 | async-start | bytes 2359296 | tf_op jit(solution)/shard_map/reduce_scatter | solution.py:50
  653.0 271.5 %reduce-scatter.30.cloned.1.call-start = ((), (), s32[]{:S(2)}) async-start(), calls=%async_computation.28 | async-start | bytes 1966080 | tf_op jit(solution)/shard_map/reduce_scatter | solution.py:161
  781.8 13.6 %all-to-all-start.2 = ((bf16[8,32,1024]{2,1,0:T(8,128)(2,1)}), bf16[8,32,1024]{2,1,0:T(8,128)(2,1)S(1)}, u32[]{:S(2)}, u32[]{:S(2)}) async-start(bf16[8,32,1024]{2,1,0:T(8,128)(2,1)} %dynamic-slice_bitcast_fusion.1), calls=%async_computation.11 | async-start | bytes 1048576 | tf_op jit(solution)/shard_map/all_to_all | solution.py:162
  795.4 14.9 %all-to-all-start.3 = ((bf16[8,32,1024]{2,1,0:T(8,128)(2,1)}), bf16[8,32,1024]{2,1,0:T(8,128)(2,1)S(1)}, u32[]{:S(2)}, u32[]{:S(2)}) async-start(bf16[8,32,1024]{2,1,0:T(8,128)(2,1)} %dynamic-slice_bitcast_fusion), calls=%async_computation.12 | async-start | bytes 1048576 | tf_op jit(solution)/shard_map/all_to_all | solution.py:162
  798.9 255.1 %all-reduce.8.cloned.1.call-start = ((), (), s32[]{:S(2)}) async-start(), calls=%async_computation.30 | async-start | bytes 196608 | tf_op jit(solution)/shard_map/psum | solution.py:188
  (70 other events, 2218.5 us)
Sparse Core Ops, SparseCore 0:
  15.7 46.0 all-gather.16
  64.3 29.9 all-gather.14
  108.6 41.1 reduce-scatter.15
  151.7 23.5 all-gather.30
  177.7 27.8 all-gather.18
  214.7 41.2 reduce-scatter.17
  258.1 44.3 all-gather.22
  304.9 28.2 all-gather.20
  335.3 44.3 all-gather.24
  381.4 28.2 all-gather.32
  421.9 41.1 reduce-scatter.21
  466.7 41.2 reduce-scatter.19
  510.9 27.8 all-gather.26
  550.2 41.1 reduce-scatter.23
  595.7 27.8 all-gather.28
  626.0 153.1 all-reduce.9
  782.8 38.5 reduce-scatter.27
  823.6 18.5 reduce-scatter.31
  845.4 42.5 reduce-scatter.25
  890.3 34.1 reduce-scatter.29
  931.6 122.3 all-reduce.7

commit v2 on v1

v2 whole, which is shorter than its diff:
```python
import functools

import jax
import jax.numpy as jnp
from jax import lax
from jax.experimental import pallas as pl
from jax.experimental.pallas import tpu as pltpu
from jax.sharding import PartitionSpec as P

D = 1024
HD = 64
LANES = 128
TILE = 256
EPS = 1e-05
NEG = -1e30
SCALE = HD ** (-0.5)
bf = jnp.bfloat16
f32 = jnp.float32
ORDER = (0, 1, 2, 5, 6, 3, 7, 4)


def dot(a, b):
    return jnp.dot(a, b, preferred_element_type=f32)


def dot_t(a, b):
    return lax.dot_general(a, b, (((1,), (1,)), ((), ())), preferred_element_type=f32)


def t_dot(a, b):
    return lax.dot_general(a, b, (((0,), (0,)), ((), ())), preferred_element_type=f32)


def normed(value):
    centred = value - jnp.mean(value, axis=-1, keepdims=True)
    inv = lax.rsqrt(jnp.mean(centred * centred, axis=-1, keepdims=True) + EPS)
    return centred * inv, inv


def norm_back(value, gain, grad):
    hat, inv = normed(value)
    scaled = grad * gain
    back = inv * (
        scaled
        - jnp.mean(scaled, axis=-1, keepdims=True)
        - hat * jnp.mean(scaled * hat, axis=-1, keepdims=True)
    )
    return back, jnp.sum(grad * hat, axis=0, keepdims=True), jnp.sum(grad, axis=0, keepdims=True)


def gelu_parts(u):
    e = jnp.exp(-0.5 * u * u)
    t = 1.0 / (1.0 + (0.3275911 * 2.0**-0.5) * jnp.abs(u))
    poly = 0.5 * 1.061405429
    for term in (-1.453152027, 1.421413741, -0.284496736, 0.254829592):
        poly = poly * t + 0.5 * term
    tail = poly * t * e
    cdf = jnp.where(u >= 0.0, 1.0 - tail, tail)
    return cdf, cdf + u * (e * 0.3989422804014327)


def subsets(items):
    out = [()]
    for item in items:
        out = out + [s + (item,) for s in out]
    return sorted(out, key=len)


class Net:
    def __init__(self, n, nz, send, recv):
        self.n, self.nz = n, nz
        self.c = lax.axis_index("ctx")
        self.z = lax.axis_index("fsdp")
        self.send, self.recv = send, recv
        self.used = 0
        self.named = {}
        self.sent = []
        self.hops = []
        bit = n // 2
        while bit > 1:
            self.hops.append(bit)
            bit //= 2
        self.delta = {b: b - 2 * b * ((self.c // b) % 2) for b in self.hops + [1]}

    def slots(self, count):
        first = self.used
        self.used += count
        return first

    def slot(self, *key):
        if key not in self.named:
            self.named[key] = self.slots(1)
        return self.named[key]

    def at(self, places):
        index = self.c
        for place in places:
            index = index + self.delta[place]
        return index

    def copy(self, src, dst, slot, ctx=None, fsdp=None):
        return pltpu.make_async_remote_copy(
            src_ref=src,
            dst_ref=dst,
            send_sem=self.send.at[slot],
            recv_sem=self.recv.at[slot],
            device_id=(self.c if ctx is None else ctx, self.z if fsdp is None else fsdp),
            device_id_type=pl.DeviceIdType.MESH,
        )

    def go(self, *args, **kw):
        made = self.copy(*args, **kw)
        made.start()
        self.sent.append(made)

    def arrived(self, ref, slot):
        self.copy(ref, ref, slot).wait_recv()

    def drain(self):
        for made in self.sent:
            made.wait_send()
        self.sent = []

    def greet(self):
        barrier = pltpu.get_barrier_semaphore()
        for d in range(1, self.n):
            pl.semaphore_signal(
                barrier, inc=1, device_id=(lax.rem(self.c + d, self.n), self.z), device_id_type=pl.DeviceIdType.MESH
            )
        for d in range(1, self.nz):
            pl.semaphore_signal(
                barrier, inc=1, device_id=(self.c, lax.rem(self.z + d, self.nz)), device_id_type=pl.DeviceIdType.MESH
            )
        pl.semaphore_wait(barrier, self.n + self.nz - 2)

    def cuts(self, columns):
        count = max(1, len(self.hops))
        units = columns // LANES
        out, first = [], 0
        for k in range(count):
            size = (units * (k + 1) // count - units * k // count) * LANES
            out.append(pl.ds(first, size))
            first += size
        return out

    def turned(self, k):
        return self.hops[k:] + self.hops[:k]


class Gather:
    def __init__(self, net, buf, pool):
        self.net, self.buf = net, buf
        self.parts = net.cuts(buf.shape[2])
        self.sent = []
        self.slot = {}
        self.slot["own"] = net.slot(pool, "own")
        for k in range(len(self.parts)):
            for s in subsets(net.turned(k)):
                if s:
                    self.slot[k, s, "hop"] = net.slot(pool, k, s, "hop")
                    self.slot[k, s, "core"] = net.slot(pool, k, s, "core")

    def go(self, *args, **kw):
        made = self.net.copy(*args, **kw)
        made.start()
        self.sent.append(made)

    def drain(self):
        for made in self.sent:
            made.wait_send()
        self.sent = []

    def ref(self, k, s):
        return self.buf.at[self.net.at(s), :, self.parts[k]]

    def forward(self, k, s, core):
        net = self.net
        order = net.turned(k)
        later = order[order.index(s[-1]) + 1:] if s else order
        for hop in later:
            ref = self.ref(k, s)
            self.go(ref, ref, self.slot[k, s + (hop,), "hop"], ctx=net.at((hop,)))
        if core:
            ref = self.ref(k, s)
            self.go(ref, ref, self.slot[k, s, "core"], ctx=net.at((1,)))

    def start(self):
        net = self.net
        for k in range(len(self.parts)):
            if net.hops:
                self.forward(k, (), False)
        own = self.buf.at[net.c]
        self.go(own, own, self.slot["own"], ctx=net.at((1,)))

    def level(self, m):
        net = self.net
        for k in range(len(self.parts)):
            for s in subsets(net.turned(k)):
                if len(s) == m:
                    net.arrived(self.ref(k, s), self.slot[k, s, "hop"])
                    self.forward(k, s, True)

    def levels(self):
        for m in range(1, len(self.net.hops) + 1):
            self.level(m)

    def done(self):
        net = self.net
        net.arrived(self.buf.at[net.at((1,))], self.slot["own"])
        for k in range(len(self.parts)):
            for s in subsets(net.turned(k)):
                if s:
                    net.arrived(self.ref(k, s + (1,)), self.slot[k, s, "core"])

    def finish(self):
        self.levels()
        self.done()


class Scatter:
    def __init__(self, net, part, came, pool):
        self.net, self.part, self.came = net, part, came
        self.parts = net.cuts(part.shape[2])
        self.sets = subsets(net.hops)[::-1]
        if (pool, "base") not in net.named:
            net.named[pool, "base"] = net.slots(len(self.sets))
        self.base = net.named[pool, "base"]
        self.slot = {}
        for k in range(len(self.parts)):
            for step in range(len(net.hops)):
                for s in subsets(net.turned(k)[step:]):
                    if net.turned(k)[step] in s:
                        self.slot[k, s] = net.slot(pool, k, s)
        self.sent = []

    def go(self, *args, **kw):
        made = self.net.copy(*args, **kw)
        made.start()
        self.sent.append(made)

    def chip(self, k):
        net = self.net
        count = len(net.hops)
        index = 0
        turn = len(self.sets) - 1 - k
        for j, hop in enumerate(net.hops):
            far = (turn // (2 ** (count - 1 - j))) % 2
            index = index + hop * (((net.c // hop) + far) % 2)
        return index

    def sets_of(self, k):
        net = self.net
        count = len(net.hops)
        turn = len(self.sets) - 1 - k
        return tuple(hop for j, hop in enumerate(net.hops) if (turn // (2 ** (count - 1 - j))) % 2)

    def core_copy(self, k):
        net = self.net
        first = self.chip(k)
        mine = lax.rem(net.c, 2)
        return net.copy(
            self.part.at[first + 1 - mine], self.came.at[first + mine], self.base + k, ctx=net.at((1,))
        )

    def push(self, k):
        self.core_copy(k).start()

    def fold(self):
        net = self.net
        part, came = self.part, self.came
        for k in range(len(self.sets)):
            s = self.sets_of(k)
            mine = net.at(s)
            other = net.at(s + (1,))
            net.arrived(came.at[other], self.base + k)
            part[mine] = (part[mine].astype(f32) + came[other].astype(f32)).astype(bf)
            for p in range(len(self.parts)):
                self.onward(p, 0, s)

    def onward(self, p, step, s):
        net = self.net
        order = net.turned(p)
        if step < len(order) and order[step] in s:
            key = tuple(h for h in order if h in s)
            rest = tuple(h for h in s if h != order[step])
            cut = self.parts[p]
            self.go(
                self.part.at[net.at(s), :, cut],
                self.came.at[net.at(rest), :, cut],
                self.slot[p, key],
                ctx=net.at((order[step],)),
            )

    def reduce(self, result):
        net = self.net
        part, came = self.part, self.came
        count = len(net.hops)
        for step in range(count):
            for p in range(len(self.parts)):
                order = net.turned(p)
                cut = self.parts[p]
                for s in subsets(order[step + 1:])[::-1]:
                    far = s + (order[step],)
                    key = tuple(h for h in order if h in far)
                    net.arrived(came.at[net.at(far), :, cut], self.slot[p, key])
                    total = part[net.at(s), :, cut].astype(f32) + came[net.at(far), :, cut].astype(f32)
                    if step == count - 1:
                        result(cut, total)
                    else:
                        part[net.at(s), :, cut] = total.astype(bf)
                        self.onward(p, step + 1, s)
        if not count:
            result(slice(None), part[net.c].astype(f32))

    def drain(self):
        for k in range(len(self.sets)):
            self.core_copy(k).wait_send()
        for made in self.sent:
            made.wait_send()
        self.sent = []


def count_slots(n, nz):
    hops = n.bit_length() - 2
    trees = 1 + max(1, hops) * 2 * (2**hops - 1)
    sums = 2**hops + max(1, hops) * (2**hops - 1)
    return 2 * trees + 2 * sums + 12 * (nz - 1) + 6 * (n - 1) + n.bit_length() + nz.bit_length() - 2


def layer(dims, *refs):
    (n, nz, t, te, w, fw, hpd) = dims
    (x_ref, e_ref, g_ref, segd_ref, segs_ref, wsl_ref, up_ref, down_ref, vec_ref,
     mixed_ref, gtok_ref, genc_ref, fu, fd, fas, fac, fos, foc, vt, hold1, hold2,
     n1x, ex, n2f, wbuf, wo, wup, wdown,
     qa1, ka1, v1, vt1, ot1, ob1, lse1, qa2, ka2, v2, vt2, ot2, ob2, lse2,
     x1, x2, pa, ra, pm, rm, dy2f,
     act, du, gu, gd, gas, gac, gos, goc, ru, rd, ras, rac, ros, roc,
     vcame, dlt, dqacc, bias_ref, bup_ref,
     send, recv, local) = refs
    length, lenc = n * t, n * te
    share = D // (n * nz)
    dz = D // nz
    nq, nk2 = length // TILE, lenc // TILE
    nbt, nbe = TILE // t, TILE // te
    net = Net(n, nz, send, recv)
    c, z = net.c, net.z
    lane = lax.broadcasted_iota(jnp.int32, (1, LANES), 1)

    dqkv, dq2, dkv2 = act.at[:, pl.ds(0, 384)], act.at[:, pl.ds(0, LANES)], act.at[pl.ds(0, lenc), pl.ds(LANES, 256)]
    dom = [du.at[:, pl.ds(h * LANES, LANES)] for h in range(hpd)]
    dx = gtok_ref

    def wor_of(j, cc):
        return pm.at[cc, pl.ds(0, w), pl.ds(j * LANES, LANES)]

    wide = -(-n * LANES // D)

    def row(k):
        return vec_ref[k:k + 1, :]

    def into(ref):
        def store(cut, total):
            ref[:, cut] = total
        return store

    zrows = pl.ds(pl.multiple_of(z * dz, dz), dz)
    fcols = pl.ds(pl.multiple_of(c * fw, LANES), fw)

    def local_copy(src, dst, k):
        made = pltpu.make_async_copy(src, dst, local.at[k])
        made.start()
        return made

    if w == LANES:
        own_cols = [
            local_copy(
                wsl_ref.at[:, pl.ds(pl.multiple_of(block * D + c * LANES, LANES), LANES)],
                wbuf.at[zrows, pl.ds(k * LANES, LANES)], k)
            for k, block in enumerate(ORDER)
        ]
    else:
        own_cols = [local_copy(wsl_ref, wbuf.at[zrows, :], 0)]
    own_feed = [
        local_copy(up_ref.at[:, fcols], wup.at[zrows, :], 8),
        local_copy(down_ref.at[:, fcols], wdown.at[zrows, :], 9),
    ]
    net.greet()

    groups = ((0, 384), (384, 256), (640, 256), (896, 128))
    wslots = [net.slots(nz - 1) - 1 for _ in groups]
    upslot, downslot = net.slots(nz - 1) - 1, net.slots(nz - 1) - 1
    def push_z(src, dst, slot):
        for d in range(1, nz):
            net.go(src, dst, slot + d, fsdp=lax.rem(z + d, nz))

    def await_z(dst_of, slot):
        for d in range(1, nz):
            net.arrived(dst_of(lax.rem(z + nz - d, nz)), slot + d)

    def weight_rows(zz, k):
        first, size = groups[k]
        return wbuf.at[pl.ds(pl.multiple_of(zz * dz, dz), dz), pl.ds(first, size)]

    def push_weights(k):
        first, size = groups[k]
        push_z(weight_rows(z, k), weight_rows(z, k), wslots[k])

    for made in own_cols:
        made.wait()
    push_weights(0)

    hat, _ = normed(x_ref[...].astype(f32))
    n1x[c, :, pl.ds(0, D)] = (hat * row(0) + row(1)).astype(bf)

    def hot(seg, rows):
        place = lax.broadcasted_iota(jnp.int32, (LANES, rows), 0) % HD
        return jnp.where(place == seg[...], 1.0, 0.0).T.astype(bf)

    n1x[c, :, pl.ds(D, LANES)] = hot(segd_ref, t)
    gat1 = Gather(net, n1x, "main")
    gat1.start()
    ex[c, :, pl.ds(0, D)] = e_ref[...]
    ex[c, :, pl.ds(D, LANES)] = hot(segs_ref, te)
    for k in range(1, len(groups)):
        push_weights(k)
    vt[...] = jnp.zeros_like(vt)
    bias_ref[...] = jnp.zeros_like(bias_ref)
    for k, line in enumerate((6, 7, 9, 10)):
        own = vec_ref[line:line + 1, 0:w]
        for cc in range(1, n):
            own = jnp.where(c == cc, vec_ref[line:line + 1, cc * w:(cc + 1) * w], own)
        bias_ref[k:k + 1, 0:w] = own
    own = vec_ref[13:14, 0:fw]
    for cc in range(1, n):
        line, first = 13 + cc * fw // D, cc * fw % D
        own = jnp.where(c == cc, vec_ref[line:line + 1, first:first + fw], own)
    bup_ref[0:1, :] = own
    vt[8:9, :] = jnp.sum(g_ref[...].astype(f32), axis=0, keepdims=True)
    gat1.levels()
    gate = Gather(net, ex, "side")
    gate.start()
    gat1.done()
    await_z(lambda zz: weight_rows(zz, 0), wslots[0])

    def tile_of(buf, i, per, columns):
        return buf[pl.ds(i * per, per), :, columns].reshape(TILE, columns.size)

    head_of = lane // HD

    def put_q(qa, q, oh, rows):
        q = (q.astype(bf).astype(f32) * SCALE).astype(bf)
        for h in range(hpd):
            qa[h, rows, :] = jnp.where(head_of == h, q, oh)

    def put_k(ka, k, oh, rows):
        k = k.astype(bf)
        pen = ((oh.astype(f32) - 1.0) * -NEG).astype(bf)
        for h in range(hpd):
            ka[h, rows, :] = jnp.where(head_of == h, k, pen)

    def put_v(v, vt_ref, value, rows, i):
        value = value.astype(bf)
        v[rows, :] = value
        vt_ref[i] = value.astype(f32).T.astype(bf)

    def tile_rows(i):
        return pl.ds(pl.multiple_of(i * TILE, TILE), TILE)

    def qkv_tile(i, _):
        rows = tile_rows(i)
        got = dot(tile_of(n1x, i, nbt, pl.ds(0, D)), wbuf[:, 0:384])
        oh = tile_of(n1x, i, nbt, pl.ds(D, LANES))
        put_q(qa1, got[:, 0:128] + bias_ref[0:1, :], oh, rows)
        put_k(ka1, got[:, 128:256], oh, rows)
        put_v(v1, vt1, got[:, 256:384] + bias_ref[1:2, :], rows, i)
        return _

    lax.fori_loop(0, nq, qkv_tile, 0)

    gf, n3f, dy1f = n1x.at[:, :, pl.ds(0, D)], n2f, n2f

    away1 = local_copy(gf, hold1, 10)

    push_z(up_ref.at[:, fcols], wup.at[zrows, :], upslot)
    push_z(down_ref.at[:, fcols], wdown.at[zrows, :], downslot)

    def attend(qa, ka, vt_ref, ot, ob, lse, keys, causal):
        def one(j, _):
            qrows = tile_rows(j)

            def step(i, state, diagonal):
                out = []
                for h in range(hpd):
                    top, total, acc = state[h]
                    s = dot_t(ka[h, tile_rows(i), :], qa[h, qrows, :])
                    if diagonal:
                        kp = lax.broadcasted_iota(jnp.int32, (TILE, TILE), 0)
                        qp = lax.broadcasted_iota(jnp.int32, (TILE, TILE), 1)
                        s = jnp.where(kp <= qp, s, NEG)
                    new = jnp.maximum(top, jnp.max(s, axis=0, keepdims=True))
                    p = jnp.exp(s - new)
                    fix = jnp.exp(top - new)
                    total = total * fix + jnp.sum(p, axis=0, keepdims=True)
                    acc = acc * fix + dot(vt_ref[i, pl.ds(h * HD, HD), :], p.astype(bf))
                    out.append((new, total, acc))
                return tuple(out)

            state = tuple(
                (jnp.full((1, TILE), -3e38, f32), jnp.zeros((1, TILE), f32), jnp.zeros((HD, TILE), f32))
                for _ in range(hpd)
            )
            if causal:
                state = step(j, state, True)
                state = lax.fori_loop(0, j, lambda i, st: step(i, st, False), state)
            else:
                state = lax.fori_loop(0, keys, lambda i, st: step(i, st, False), state)
            for h in range(hpd):
                top, total, acc = state[h]
                ot[j, pl.ds(h * HD, HD), :] = acc * (1.0 / total)
                lse[j, h:h + 1, :] = top + jnp.log(total)
            ob[qrows, :] = ot[j].T.astype(bf)
            return _

        if hpd * HD < LANES:
            ot[...] = jnp.zeros_like(ot)
        lax.fori_loop(0, nq, one, 0)

    attend(qa1, ka1, vt1, ot1, ob1, lse1, nq, True)

    await_z(lambda zz: weight_rows(zz, 1), wslots[1])
    await_z(lambda zz: weight_rows(zz, 2), wslots[2])
    oslots = [net.slots(n - 1) - 1, net.slots(n - 1) - 1]

    def out_rows(j, cc):
        return wbuf.at[pl.ds(pl.multiple_of(cc * w, w), w), pl.ds(640 + j * LANES, LANES)]

    for j in range(2):
        for d in range(1, n):
            peer = lax.rem(c + d, n)
            net.go(out_rows(j, peer), wor_of(j, c), oslots[j] + d, ctx=peer)
        wor_of(j, c)[...] = wbuf[pl.ds(pl.multiple_of(c * w, w), w), pl.ds(640 + j * LANES, LANES)]

    def await_out(j):
        for d in range(1, n):
            net.arrived(wor_of(j, lax.rem(c + n - d, n)), oslots[j] + d)
        if w < LANES:
            wo[j] = jnp.zeros((LANES, D), bf)
        wo[j, pl.ds(0, w), :] = jnp.concatenate(
            [pm[cc, pl.ds(0, w), pl.ds(j * LANES, LANES)][:, :w] for cc in range(n)], axis=-1)

    gate.finish()
    await_out(0)

    def partial(scat, rows_of, weight_of, per):
        def one(k, _):
            first = scat.chip(k)
            scat.part[pl.ds(first, 2)] = weight_of(rows_of(first)).astype(bf).reshape(2, per, D)
            scat.push(k)
            return _

        lax.fori_loop(0, n // 2, one, 0)

    def flat(buf, per):
        return lambda first: buf[pl.ds(pl.multiple_of(first * per, 2 * per), 2 * per), :]

    rs1 = Scatter(net, pa, ra, "sum")
    partial(rs1, flat(ob1, t), lambda rows: dot(rows, wo[0]), t)

    def kv2_tile(i, _):
        rows = tile_rows(i)
        got = dot(tile_of(ex, i, nbe, pl.ds(0, D)), wbuf[:, 384:640])
        oh = tile_of(ex, i, nbe, pl.ds(D, LANES))
        put_k(ka2, got[:, 0:128], oh, rows)
        put_v(v2, vt2, got[:, 128:256] + bias_ref[3:4, :], rows, i)
        return _

    rs1.fold()
    lax.fori_loop(0, nk2, kv2_tile, 0)
    rs1.reduce(into(x1))
    x1[...] = x_ref[...].astype(f32) + (x1[...] + row(8))
    hat, _ = normed(x1[...])
    n2f[c] = (hat * row(2) + row(3)).astype(bf)
    gat1.drain()
    away1.wait()
    gat2 = Gather(net, n2f, "main")
    gat2.start()
    rs1.drain()
    gate.drain()
    await_out(1)
    await_z(lambda zz: weight_rows(zz, 3), wslots[3])
    gat2.finish()
    gf[c] = g_ref[...]
    gatg = Gather(net, gf, "side")
    gatg.start()

    def q2_tile(i, _):
        got = dot(tile_of(n2f, i, nbt, pl.ds(0, D)), wbuf[:, 896:1024])
        put_q(qa2, got + bias_ref[2:3, :], tile_of(n1x, i, nbt, pl.ds(D, LANES)), tile_rows(i))
        return _

    lax.fori_loop(0, nq, q2_tile, 0)
    away2 = local_copy(n2f, hold2, 11)
    gatg.level(1)
    attend(qa2, ka2, vt2, ot2, ob2, lse2, nk2, False)
    away2.wait()
    gat2.drain()
    rs2 = Scatter(net, pa, ra, "sum")
    partial(rs2, flat(ob2, t), lambda rows: dot(rows, wo[1]), t)
    for m in range(2, len(net.hops) + 1):
        gatg.level(m)
    rs2.fold()
    rs2.reduce(into(x2))
    x2[...] = x1[...] + (x2[...] + row(11))
    hat, _ = normed(x2[...])
    n3f[c] = (hat * row(4) + row(5)).astype(bf)
    gat3 = Gather(net, n3f, "main")
    gat3.start()
    rs2.drain()
    gatg.done()
    for made in own_feed:
        made.wait()
    gat3.finish()
    await_z(lambda zz: wup.at[pl.ds(pl.multiple_of(zz * dz, dz), dz), :], upslot)
    await_z(lambda zz: wdown.at[pl.ds(pl.multiple_of(zz * dz, dz), dz), :], downslot)

    rs3 = Scatter(net, pa, ra, "sum")
    rsm = Scatter(net, pm, rm, "sum2")
    fc = min(fw, 512)

    def feed_tile(k, sums):
        first = rs3.chip(k)
        rows = pl.ds(pl.multiple_of(first * t, 2 * t), 2 * t)
        left = n3f[pl.ds(first, 2)].reshape(2 * t, D)
        grad = gf[pl.ds(first, 2)].reshape(2 * t, D)
        out = []
        for f in range(fw // fc):
            cols = pl.ds(f * fc, fc)
            u = dot(left, wup[:, cols]) + bup_ref[0:1, cols]
            cdf, slope = gelu_parts(u)
            act[rows, cols] = (u * cdf).astype(bf)
            low = (dot(grad, wdown[:, cols]) * slope).astype(bf)
            du[rows, cols] = low
            out.append(sums[f] + jnp.sum(low.astype(f32), axis=0, keepdims=True))
        pa[pl.ds(first, 2)] = dot_t(du[rows, :], wup[...]).astype(bf).reshape(2, t, D)
        rs3.push(k)
        return tuple(out)

    sums = lax.fori_loop(0, n // 2, feed_tile, tuple(jnp.zeros((1, fc), f32) for _ in range(fw // fc)))
    for f in range(fw // fc):
        for cc in range(n):
            place = cc * fw + f * fc
            line = 9 + 4 * wide + place // D
            vt[line:line + 1, pl.ds(place % D, fc)] = jnp.where(c == cc, sums[f], 0.0)
    rs3.fold()
    partial(rsm, flat(act, t), lambda rows: dot_t(rows, wdown[...]), t)
    rsm.fold()

    per = TILE // (share * nz)

    def weight_grad(left_of, right, out, columns):
        def one(r, _):
            got = t_dot(left_of(tile_rows(r)), right())
            for k in range(TILE // share):
                out[k % nz, r * per + k // nz, :, columns] = got[k * share:(k + 1) * share].astype(bf)
            return _

        lax.fori_loop(0, D // TILE, one, 0)

    def whole(buf, rows):
        return lambda cols: buf[:, :, cols].reshape(rows, TILE)

    zslots = [net.slots(nz - 1) - 1 for _ in range(6)]

    def push_grad(mine, came, k):
        for d in range(1, nz):
            peer = lax.rem(z + d, nz)
            net.go(mine.at[peer], came.at[z], zslots[k] + d, fsdp=peer)

    def sum_grad(mine, came, k):
        total = mine[z].astype(f32)
        for d in range(1, nz):
            peer = lax.rem(z + nz - d, nz)
            net.arrived(came.at[peer], zslots[k] + d)
            total = total + came[peer].astype(f32)
        return total.astype(bf)

    weight_grad(whole(n3f, length), lambda: du[...], gu, pl.ds(0, fw))
    push_grad(gu, ru, 0)
    gat3.drain()
    gatg.drain()
    rs3.reduce(into(dx))
    back, gain_g, shift_g = norm_back(x2[...], row(4), dx[...])
    vt[4:5, :] = gain_g
    vt[5:6, :] = shift_g
    dx[...] = g_ref[...].astype(f32) + back
    dy = dx[...].astype(bf)
    dy2f[c] = dy
    gat4 = Gather(net, dy2f, "main")
    gat4.start()
    vt[7:8, :] = jnp.sum(dy.astype(f32), axis=0, keepdims=True)
    rs3.drain()
    gat4.levels()
    weight_grad(whole(gf, length), lambda: act[...], gd, pl.ds(0, fw))
    push_grad(gd, rd, 1)
    back2 = local_copy(hold2, gf, 12)

    def store_mixed(cut, total):
        mixed_ref[:, cut] = (x2[:, cut] + (total + vec_ref[12:13, cut])).astype(bf)

    rsm.reduce(store_mixed)
    gat4.done()

    def attend_back(qa, ka, v, ot, lse, dyf, out_w, keys, causal, dq_ref, dq_cols, dkv_ref, dk_cols, dv_cols):
        def grads(i, _):
            rows = tile_rows(i)
            low = dot_t(tile_of(dyf, i, nbt, pl.ds(0, D)), out_w[...]).astype(bf)
            for h in range(hpd):
                dom[h][rows, :] = jnp.where(head_of == h, low, jnp.zeros_like(low))
            prod = low.astype(f32).T * ot[i]
            for h in range(hpd):
                dlt[i, h:h + 1, :] = jnp.sum(prod[h * HD:(h + 1) * HD], axis=0, keepdims=True)
            dqacc[rows, :] = jnp.zeros((TILE, LANES), f32)
            return _

        lax.fori_loop(0, nq, grads, 0)

        def one(i, _):
            krows = tile_rows(i)

            def step(j, state, diagonal):
                qrows = tile_rows(j)
                dv, dks = state
                new_dks, dqs = [], []
                for h in range(hpd):
                    s = dot_t(ka[h, krows, :], qa[h, qrows, :])
                    p = jnp.exp(s - lse[j, h:h + 1, :])
                    if diagonal:
                        kp = lax.broadcasted_iota(jnp.int32, (TILE, TILE), 0)
                        qp = lax.broadcasted_iota(jnp.int32, (TILE, TILE), 1)
                        p = jnp.where(kp <= qp, p, 0.0)
                    dp = dot_t(v[krows, :], dom[h][qrows, :])
                    ds = (p * (dp - dlt[j, h:h + 1, :])).astype(bf)
                    dv = dv + dot(p.astype(bf), dom[h][qrows, :])
                    new_dks.append(dks[h] + dot(ds, qa[h, qrows, :]))
                    dqs.append(t_dot(ds, ka[h, krows, :]))
                dq = jnp.where(head_of == 0, dqs[0], dqs[-1] if hpd > 1 else 0.0)
                dqacc[qrows, :] = dqacc[qrows, :] + dq
                return dv, tuple(new_dks)

            zero = jnp.zeros((TILE, LANES), f32)
            state = (zero, tuple(zero for _ in range(hpd)))
            if causal:
                state = step(i, state, True)
                state = lax.fori_loop(i + 1, nq, lambda j, st: step(j, st, False), state)
            else:
                state = lax.fori_loop(0, nq, lambda j, st: step(j, st, False), state)
            dv, dks = state
            dk = jnp.where(head_of == 0, dks[0], dks[-1] if hpd > 1 else 0.0)
            dkv_ref[krows, dk_cols] = dk.astype(bf)
            dkv_ref[krows, dv_cols] = dv.astype(bf)
            return _

        lax.fori_loop(0, keys, one, 0)

        def close(i, _):
            rows = tile_rows(i)
            dq_ref[rows, dq_cols] = (dqacc[rows, :] * SCALE).astype(bf)
            return _

        lax.fori_loop(0, nq, close, 0)

    def head_sum(k, ref, cols):
        own = jnp.sum(ref[:, cols].astype(f32), axis=0, keepdims=True)
        for cc in range(n):
            line = 9 + k * wide + cc * LANES // D
            vt[line:line + 1, pl.ds(cc * LANES % D, LANES)] = jnp.where(c == cc, own, 0.0)

    first3 = [pl.ds(k * LANES, LANES) for k in range(3)]
    attend_back(qa2, ka2, v2, ot2, lse2, dy2f, wo.at[1], nk2, False, dq2, first3[0], dkv2, first3[0], first3[1])
    rs4 = Scatter(net, pa, ra, "sum")
    partial(rs4, flat(dq2, t), lambda rows: dot_t(rows, wbuf[:, 896:1024]), t)
    rs4.fold()

    weight_grad(whole(ex, lenc), lambda: dkv2[...], gac, pl.ds(0, 256))
    back2.wait()
    weight_grad(whole(gf, length), lambda: dq2[...], gac, pl.ds(256, 128))
    back1 = local_copy(hold1, gf, 13)
    push_grad(gac, rac, 2)

    def out_grad(ob, dyf, out):
        for cut in (0, 1):
            cols = pl.ds(cut * (D // 2), D // 2)
            got = t_dot(ob[...], dyf[:, :, cols].reshape(length, D // 2))
            for k in range(nz):
                out[k, :, cols] = got[k * share:(k + 1) * share].astype(bf)

    rs4.reduce(into(x2))
    back, gain_g, shift_g = norm_back(x1[...], row(2), x2[...])
    vt[2:3, :] = gain_g
    vt[3:4, :] = shift_g
    dx[...] = dx[...] + back
    dy = dx[...].astype(bf)
    dy1f[c] = dy
    gat4.drain()
    gat5 = Gather(net, dy1f, "main")
    gat5.start()
    vt[6:7, :] = jnp.sum(dy.astype(f32), axis=0, keepdims=True)
    head_sum(2, dq2, first3[0])
    head_sum(3, dkv2, first3[1])
    rs4.drain()
    rsm.drain()
    rse = Scatter(net, pm.at[:, pl.ds(0, te), :], rm.at[:, pl.ds(0, te), :], "sum2")
    partial(rse, flat(dkv2, te), lambda rows: dot_t(rows, wbuf[:, 384:640]), te)
    gat5.levels()
    rse.fold()
    out_grad(ob2, dy2f, goc)
    push_grad(goc, roc, 3)
    rse.reduce(into(genc_ref))
    gat5.done()
    attend_back(qa1, ka1, v1, ot1, lse1, dy1f, wo.at[0], nq, True, dqkv, first3[0], dqkv, first3[1], first3[2])
    rs5 = Scatter(net, pa, ra, "sum")
    partial(rs5, flat(dqkv, t), lambda rows: dot_t(rows, wbuf[:, 0:384]), t)
    rs5.fold()
    back1.wait()
    weight_grad(whole(gf, length), lambda: dqkv[...], gas, pl.ds(0, 384))
    push_grad(gas, ras, 4)
    out_grad(ob1, dy1f, gos)
    push_grad(gos, ros, 5)
    rs5.reduce(into(x2))
    back, gain_g, shift_g = norm_back(x_ref[...].astype(f32), row(0), x2[...])
    vt[0:1, :] = gain_g
    vt[1:2, :] = shift_g
    gtok_ref[...] = dx[...] + back
    head_sum(0, dqkv, first3[0])
    head_sum(1, dqkv, first3[2])

    vslots = net.slots(vcame.shape[0])
    pairs = [("ctx", b) for b in net.hops + [1]] + [("fsdp", 1 << k) for k in range(nz.bit_length() - 1)]

    def swap(k):
        axis, b = pairs[k]
        own = c if axis == "ctx" else z
        peer = own + b - 2 * b * ((own // b) % 2)
        made = net.copy(vt, vcame.at[k], vslots + k, **{axis: peer})
        made.start()
        return made

    def merge(k, made):
        made.wait_send()
        net.arrived(vcame.at[k], vslots + k)
        vt[...] = vt[...] + vcame[k]

    def exchange(mine, came, k, out):
        slot = net.slots(n - 1) - 1
        mine[z] = sum_grad(mine, came, k)
        out[c] = mine[z, c]
        for d in range(1, n):
            peer = lax.rem(c + d, n)
            net.go(mine.at[z, peer], out.at[c], slot + d, ctx=peer)

        def done():
            for d in range(1, n):
                net.arrived(out.at[lax.rem(c + n - d, n)], slot + d)
        return done

    waits = []
    todo = [
        lambda: waits.append(exchange(gu, ru, 0, fu)),
        lambda: waits.append(exchange(gd, rd, 1, fd)),
        lambda: waits.append(exchange(gac, rac, 2, fac)),
    ]
    for k in range(len(pairs)):
        made = swap(k)
        if todo:
            todo.pop(0)()
        merge(k, made)
    for step in todo:
        step()
    foc[...] = sum_grad(goc, roc, 3)
    waits.append(exchange(gas, ras, 4, fas))
    fos[...] = sum_grad(gos, ros, 5)
    for wait in waits:
        wait()
    rs5.drain()
    rse.drain()
    gat5.drain()
    net.drain()
    assert net.used == count_slots(n, nz)


def body(tokens, encoder, dec_seg, src_seg, attn_w, up_w, down_w, vec, cot):
    n, nz = lax.axis_size("ctx"), lax.axis_size("fsdp")
    c = lax.axis_index("ctx")
    t, te = tokens.shape[1], encoder.shape[1]
    ff = up_w.shape[1]
    w, fw = D // n, ff // n
    hpd = w // HD
    dz = D // nz
    share = D // (n * nz)
    length, lenc = n * t, n * te

    if w < LANES:
        wsl = lax.dynamic_slice_in_dim(attn_w.reshape(dz, 8, D), c * w, w, axis=2)
        wsl = jnp.stack([wsl[:, k] for k in ORDER], axis=1)
        attn_w = jnp.pad(wsl, ((0, 0), (0, 0), (0, LANES - w))).reshape(dz, 8 * LANES)

    nq, nk2 = length // TILE, lenc // TILE
    slots = count_slots(n, nz)
    dims = (n, nz, t, te, w, fw, hpd)
    wide = -(-n * LANES // D)
    vrows = -(-(9 + 4 * wide + ff // D) // 8) * 8
    steps = n.bit_length() + nz.bit_length() - 2
    out_shape = (
        jax.ShapeDtypeStruct((t, D), bf),
        jax.ShapeDtypeStruct((t, D), f32),
        jax.ShapeDtypeStruct((te, D), f32),
        jax.ShapeDtypeStruct((n, share, fw), bf),
        jax.ShapeDtypeStruct((n, share, fw), bf),
        jax.ShapeDtypeStruct((n, share, 384), bf),
        jax.ShapeDtypeStruct((n, share, 384), bf),
        jax.ShapeDtypeStruct((share, D), bf),
        jax.ShapeDtypeStruct((share, D), bf),
        jax.ShapeDtypeStruct((vrows, D), f32),
        jax.ShapeDtypeStruct((n, t, D), bf),
        jax.ShapeDtypeStruct((n, t, D), bf),
    )

    def attn_scratch(keys):
        return [
            pltpu.VMEM((hpd, length, LANES), bf), pltpu.VMEM((hpd, keys, LANES), bf), pltpu.VMEM((keys, LANES), bf),
            pltpu.VMEM((keys // TILE, LANES, TILE), bf), pltpu.VMEM((nq, LANES, TILE), f32),
            pltpu.VMEM((length, LANES), bf), pltpu.VMEM((nq, 8, TILE), f32),
        ]

    scratch = [
        pltpu.VMEM((n, t, D + LANES), bf), pltpu.VMEM((n, te, D + LANES), bf), pltpu.VMEM((n, t, D), bf),
        pltpu.VMEM((D, 8 * LANES), bf), pltpu.VMEM((2, LANES, D), bf),
        pltpu.VMEM((D, fw), bf), pltpu.VMEM((D, fw), bf),
        *attn_scratch(length), *attn_scratch(lenc),
        pltpu.VMEM((t, D), f32), pltpu.VMEM((t, D), f32),
        pltpu.VMEM((n, t, D), bf), pltpu.VMEM((n, t, D), bf), pltpu.VMEM((n, t, D), bf), pltpu.VMEM((n, t, D), bf),
        pltpu.VMEM((n, t, D), bf),
        pltpu.VMEM((length, fw), bf), pltpu.VMEM((length, fw), bf),
    ]
    for _ in range(2):
        scratch += [
            pltpu.VMEM((nz, n, share, fw), bf), pltpu.VMEM((nz, n, share, fw), bf),
            pltpu.VMEM((nz, n, share, 384), bf), pltpu.VMEM((nz, n, share, 384), bf),
            pltpu.VMEM((nz, share, D), bf), pltpu.VMEM((nz, share, D), bf),
        ]
    scratch += [
        pltpu.VMEM((steps, vrows, D), f32),
        pltpu.VMEM((nq, 8, TILE), f32), pltpu.VMEM((length, LANES), f32),
        pltpu.VMEM((8, LANES), f32), pltpu.VMEM((8, fw), f32),
        pltpu.SemaphoreType.DMA((slots,)), pltpu.SemaphoreType.DMA((slots,)), pltpu.SemaphoreType.DMA((16,)),
    ]
    vmem = pl.BlockSpec(memory_space=pltpu.VMEM)
    hbm = pl.BlockSpec(memory_space=pl.ANY)
    mixed, gtok, genc, fu, fd, fas, fac, fos, foc, vsum, _, _ = pl.pallas_call(
        functools.partial(layer, dims),
        out_shape=out_shape,
        in_specs=[vmem] * 5 + [hbm] * 3 + [vmem],
        out_specs=[vmem] * (len(out_shape) - 2) + [hbm] * 2,
        scratch_shapes=scratch,
        compiler_params=pltpu.CompilerParams(
            collective_id=0, has_side_effects=True, vmem_limit_bytes=63 * 1024 * 1024
        ),
        cost_estimate=pl.CostEstimate(flops=21_000_000_000, bytes_accessed=30_000_000, transcendentals=8_000_000),
        name="layer",
    )(tokens[0], encoder[0], cot[0], dec_seg, src_seg, attn_w, up_w, down_w, vec)

    return pl.pallas_call(
        functools.partial(closing, (n, w, fw, wide)),
        out_shape=(
            jax.ShapeDtypeStruct((1, t, D), bf), jax.ShapeDtypeStruct((1, t, D), f32),
            jax.ShapeDtypeStruct((1, te, D), f32), jax.ShapeDtypeStruct((share, 8 * D), f32),
            jax.ShapeDtypeStruct((share, ff), f32), jax.ShapeDtypeStruct((share, ff), f32),
            jax.ShapeDtypeStruct(vec.shape, f32),
        ),
        in_specs=[hbm] * 10,
        out_specs=[hbm] * 7,
        scratch_shapes=[pltpu.VMEM(a.shape, a.dtype) for a in (mixed, gtok, genc, fu, fd, fas, fac, fos, foc, vsum)] + [
            pltpu.VMEM((share, 8 * D), f32), pltpu.VMEM((share, ff), f32), pltpu.VMEM((share, ff), f32),
            pltpu.VMEM(vec.shape, f32), pltpu.SemaphoreType.DMA((17,)),
        ],
        compiler_params=pltpu.CompilerParams(vmem_limit_bytes=62 * 1024 * 1024),
        name="closing",
    )(mixed, gtok, genc, fu, fd, fas, fac, fos, foc, vsum)


def closing(dims, *refs):
    n, w, fw, wide = dims
    given, outs, kept, made, sems = refs[:10], refs[10:17], refs[17:27], refs[27:31], refs[31]
    coming = [pltpu.make_async_copy(given[k], kept[k], sems.at[k]) for k in range(10)]
    straight = [pltpu.make_async_copy(kept[k], outs[k].at[0], sems.at[10 + k]) for k in range(3)]
    going = [pltpu.make_async_copy(made[k], outs[3 + k], sems.at[13 + k]) for k in range(4)]
    for copy in coming:
        copy.start()
    for k in range(3):
        coming[k].wait()
        straight[k].start()
    kept, coming = kept[3:], coming[3:]
    fu, fd, fas, fac, fos, foc, vsum = kept
    o_attn, o_up, o_down, o_vec = made
    coming[0].wait()
    for cc in range(n):
        o_up[:, pl.ds(cc * fw, fw)] = fu[cc].astype(f32)
    going[1].start()
    coming[1].wait()
    for cc in range(n):
        o_down[:, pl.ds(cc * fw, fw)] = fd[cc].astype(f32)
    going[2].start()
    for k in range(2, 7):
        coming[k].wait()
    for block, (ref, k) in enumerate(
        ((fas, 0), (fas, 1), (fas, 2), (fos, None), (fac, 2), (fac, 0), (fac, 1), (foc, None))
    ):
        if k is None:
            got = ref[...]
        else:
            got = jnp.concatenate([ref[cc, :, pl.ds(k * LANES, LANES)][:, :w] for cc in range(n)], axis=-1)
        o_attn[:, pl.ds(block * D, D)] = got.astype(f32)
    going[0].start()

    def heads(k):
        parts = []
        for cc in range(n):
            line, first = 9 + k * wide + cc * LANES // D, cc * LANES % D
            parts.append(vsum[line:line + 1, first:first + LANES][:, :w])
        return jnp.concatenate(parts, axis=-1)

    o_vec[0:6] = vsum[0:6]
    o_vec[6:7] = heads(0)
    o_vec[7:8] = heads(1)
    o_vec[8:9] = vsum[6:7]
    o_vec[9:10] = heads(2)
    o_vec[10:11] = heads(3)
    o_vec[11:13] = vsum[7:9]
    up = 9 + 4 * wide
    o_vec[13:] = vsum[up:up + o_vec.shape[0] - 13]
    going[3].start()
    for copy in straight + going:
        copy.wait()


def solution(mesh):
    return jax.shard_map(
        body, mesh=mesh,
        in_specs=(P("fsdp", "ctx", None), P("fsdp", "ctx", None), P("fsdp", "ctx"), P("fsdp", "ctx"), P("fsdp", None),
                  P("fsdp", None), P("fsdp", None), P(), P("fsdp", "ctx", None)),
        out_specs=(P("fsdp", "ctx", None), P("fsdp", "ctx", None), P("fsdp", "ctx", None), P(("ctx", "fsdp"), None),
                   P(("ctx", "fsdp"), None), P(("ctx", "fsdp"), None), P()),
        check_vma=False,
    )
```

time: 1070 us -> 317 us (0.30)
  waiting for transfers between devices: 831 us -> 0 us
  Pallas kernels: 0 us -> 315 us
  matrix products: 101 us -> 0 us
  local copies, waits for them, and re-layouts: 42.6 us -> 0 us
  other arithmetic: 32.7 us -> 0 us
  blocking collectives: 22.6 us -> 0 us
  starting transfers between devices: 16 us -> 0 us
  between operations: 16.6 us -> 0.8 us
    pallas_call x0 -> x2, Pallas kernels: none -> 315 us  [the longest x1 312 us: body(): pl.pallas_call(functools.partial(layer, dims), out_shape=out_shape, in_sp...]
    reduce_scatter x9 -> x0, waiting for transfers between devices: 305 us -> none  [the longest x7 254 us: scatter(): lax.psum_scatter(a.astype(bf), 'ctx', scatter_dimension=0, tiled=True)]
    all_gather x10 -> x0, waiting for transfers between devices: 271 us -> none  [the longest x7 147 us: gather(): return lax.all_gather(a, 'ctx', axis=0, tiled=True)]
    psum x1 -> x0, waiting for transfers between devices: 116 us -> none  [body(): grad_vectors = lax.psum(terms, ('ctx', 'fsdp'))]
    unnamed x22 -> x0, waiting for transfers between devices: 116 us -> none
    dot_general x33 -> x0, matrix products: 101 us -> none  [the longest x7 25.4 us: dot(): return jnp.dot(a, b, preferred_element_type=f32)]
    all_to_all x4 -> x0, waiting for transfers between devices: 23.2 us -> none  [the longest x3 23.2 us: owned(): got = lax.all_to_all(summed, 'ctx', 0, 0, tiled=False)]
    reduce_sum x14 -> x0, other arithmetic: 17.1 us -> none  [the longest x3 5.76 us: csum(): return jnp.sum(a.astype(f32), axis=0)]
  transfers between devices with their start and end apart: 25 -> 0, of which waited for: 24 -> 0; matrix products, arithmetic and copies ran while one was open for 10% -> 0% of each run, Pallas kernels for 0% -> 0%
where the time goes in v2:
time: 317 us; the launch traced here: 316 us
  Pallas kernels  315 us (99%)
    pallas_call x1, Pallas kernels, body(): pl.pallas_call(functools.partial(layer, dims), out_shape=out_shape, in_sp...  312 us

profile of v2, /device:TPU:8, one launch (start us, length us, event | category | flops | bytes accessed | tf_op | source)
XLA Modules:
  0.0 315.6 jit_solution(9620622580276187583)
XLA Ops:
  0.6 311.6 %layer.1 = (bf16[128,1024]{1,0:T(8,128)(2,1)}, f32[128,1024]{1,0:T(8,128)}, f32[64,1024]{1,0:T(8,128)}, bf16[8,32,1024]{2,1,0:T(8,128)(2,1)}, bf16[8,32,1024]{2,...) custom-call(bf16[128,1024]{1,0:T(8,128)(2,1)} %bitcast.3, ...), custom_call_target="tpu_custom_call" | custom-call | flops 20999999488 | bytes 30000000 | tf_op jit(solution)/shard_map/layer/pallas_call | solution.py:959
  312.2 3.3 %closing.1 = (bf16[1,128,1024]{2,1,0:T(8,128)(2,1)}, f32[1,128,1024]{2,1,0:T(8,128)}, f32[1,64,1024]{2,1,0:T(8,128)}, f32[32,8192]{1,0:T(8,128)}, f32[32,8192]{1...) custom-call(bf16[128,1024]{1,0:T(8,128)(2,1)} %get-tuple-element.17.refs_0_, f32[128,1024]{1,0:T(8,128)} %get-tuple-element.18.refs_1_, ...), custom_call_target="tpu_custom_call" | custom-call | tf_op jit(solution)/shard_map/closing/pallas_call | solution.py:972

commit v3 on v2

--- a/solution.py
+++ b/solution.py
@@ -11,12 +11,14 @@
 HD = 64
 LANES = 128
 TILE = 256
+EXTRAS = 16
 EPS = 1e-05
 NEG = -1e30
 SCALE = HD ** (-0.5)
 bf = jnp.bfloat16
 f32 = jnp.float32
-ORDER = (0, 1, 2, 5, 6, 3, 7, 4)
+ORDER = (0, 1, 2, 3, 5, 6, 7, 4)
+OUT_AT = (384, 768)
 
 
 def dot(a, b):
@@ -67,58 +69,62 @@
 
 
 class Net:
-    def __init__(self, n, nz, send, recv):
+    def __init__(self, n, nz, q, send, recv):
         self.n, self.nz = n, nz
         self.c = lax.axis_index("ctx")
         self.z = lax.axis_index("fsdp")
         self.send, self.recv = send, recv
-        self.used = 0
+        self.used = self.extras = 0
         self.named = {}
         self.sent = []
-        self.hops = []
-        bit = n // 2
-        while bit > 1:
-            self.hops.append(bit)
-            bit //= 2
-        self.delta = {b: b - 2 * b * ((self.c // b) % 2) for b in self.hops + [1]}
+        hops = [n >> k for k in range(1, n.bit_length() - 1)]
+        self.parity = lax.rem(self.z, q)
+        self.delta = {b: b - 2 * b * ((self.c // b) % 2) for b in hops + [1]}
+        self.delta["z"] = n * (1 - 2 * self.parity)
+        self.plane = Group(self, hops, self.c)
+        self.wide = Group(self, ["z"] + hops, self.parity * n + self.c) if q == 2 else self.plane
 
     def slots(self, count):
         first = self.used
         self.used += count
         return first
 
+    def extra(self):
+        self.extras += 1
+        return self.send.shape[0] - self.extras
+
     def slot(self, *key):
         if key not in self.named:
             self.named[key] = self.slots(1)
         return self.named[key]
 
-    def at(self, places):
-        index = self.c
-        for place in places:
-            index = index + self.delta[place]
-        return index
-
-    def copy(self, src, dst, slot, ctx=None, fsdp=None):
+    def copy(self, src, dst, slot, ctx=None, fsdp=None, out=None):
         return pltpu.make_async_remote_copy(
             src_ref=src,
             dst_ref=dst,
-            send_sem=self.send.at[slot],
+            send_sem=self.send.at[slot if out is None else out],
             recv_sem=self.recv.at[slot],
             device_id=(self.c if ctx is None else ctx, self.z if fsdp is None else fsdp),
             device_id_type=pl.DeviceIdType.MESH,
         )
 
-    def go(self, *args, **kw):
+    def go(self, *args, when=None, **kw):
         made = self.copy(*args, **kw)
-        made.start()
-        self.sent.append(made)
+        if when is None:
+            made.start()
+        else:
+            pl.when(when)(made.start)
+        self.sent.append((made, when))
 
     def arrived(self, ref, slot):
         self.copy(ref, ref, slot).wait_recv()
 
     def drain(self):
-        for made in self.sent:
-            made.wait_send()
+        for made, when in self.sent:
+            if when is None:
+                made.wait_send()
+            else:
+                pl.when(when)(made.wait_send)
         self.sent = []
 
     def greet(self):
@@ -133,6 +139,34 @@
             )
         pl.semaphore_wait(barrier, self.n + self.nz - 2)
 
+
+class Group:
+    def __init__(self, net, hops, own):
+        self.net, self.hops, self.own = net, hops, own
+        self.blocks = 2 ** (len(hops) + 1)
+
+    def at(self, places):
+        index = self.own
+        for place in places:
+            index = index + self.net.delta[place]
+        return index
+
+    def peer(self, hop):
+        if hop == "z":
+            return {"fsdp": self.net.z + 1 - 2 * self.net.parity}
+        return {"ctx": self.net.c + self.net.delta[hop]}
+
+    def chip(self, turn):
+        net, count = self.net, len(self.hops)
+        index = 0
+        for j, hop in enumerate(self.hops):
+            far = (turn // (2 ** (count - 1 - j))) % 2
+            if hop == "z":
+                index = index + net.n * ((net.parity + far) % 2)
+            else:
+                index = index + hop * (((net.c // hop) + far) % 2)
+        return index
+
     def cuts(self, columns):
         count = max(1, len(self.hops))
         units = columns // LANES
@@ -148,69 +182,58 @@
 
 
 class Gather:
-    def __init__(self, net, buf, pool):
-        self.net, self.buf = net, buf
-        self.parts = net.cuts(buf.shape[2])
-        self.sent = []
+    def __init__(self, net, group, buf, pool):
+        self.net, self.group, self.buf = net, group, buf
+        self.parts = group.cuts(buf.shape[2])
+        self.out = net.slot(pool, "own")
         self.slot = {}
-        self.slot["own"] = net.slot(pool, "own")
         for k in range(len(self.parts)):
-            for s in subsets(net.turned(k)):
+            for s in subsets(group.turned(k)):
                 if s:
                     self.slot[k, s, "hop"] = net.slot(pool, k, s, "hop")
                     self.slot[k, s, "core"] = net.slot(pool, k, s, "core")
 
-    def go(self, *args, **kw):
-        made = self.net.copy(*args, **kw)
-        made.start()
-        self.sent.append(made)
+    def go(self, ref, slot, hop):
+        self.net.copy(ref, ref, slot, out=self.out, **self.group.peer(hop)).start()
 
     def drain(self):
-        for made in self.sent:
-            made.wait_send()
-        self.sent = []
+        ref = self.buf.at[pl.ds(0, self.group.blocks - 1)]
+        self.net.copy(ref, ref, self.out, out=self.out).wait_send()
 
     def ref(self, k, s):
-        return self.buf.at[self.net.at(s), :, self.parts[k]]
+        return self.buf.at[self.group.at(s), :, self.parts[k]]
 
     def forward(self, k, s, core):
-        net = self.net
-        order = net.turned(k)
+        order = self.group.turned(k)
         later = order[order.index(s[-1]) + 1:] if s else order
         for hop in later:
-            ref = self.ref(k, s)
-            self.go(ref, ref, self.slot[k, s + (hop,), "hop"], ctx=net.at((hop,)))
+            self.go(self.ref(k, s), self.slot[k, s + (hop,), "hop"], hop)
         if core:
-            ref = self.ref(k, s)
-            self.go(ref, ref, self.slot[k, s, "core"], ctx=net.at((1,)))
+            self.go(self.ref(k, s), self.slot[k, s, "core"], 1)
 
     def start(self):
-        net = self.net
         for k in range(len(self.parts)):
-            if net.hops:
+            if self.group.hops:
                 self.forward(k, (), False)
-        own = self.buf.at[net.c]
-        self.go(own, own, self.slot["own"], ctx=net.at((1,)))
+        self.go(self.buf.at[self.group.own], self.out, 1)
 
     def level(self, m):
-        net = self.net
         for k in range(len(self.parts)):
-            for s in subsets(net.turned(k)):
+            for s in subsets(self.group.turned(k)):
                 if len(s) == m:
-                    net.arrived(self.ref(k, s), self.slot[k, s, "hop"])
+                    self.net.arrived(self.ref(k, s), self.slot[k, s, "hop"])
                     self.forward(k, s, True)
 
-    def levels(self):
-        for m in range(1, len(self.net.hops) + 1):
+    def levels(self, first=1):
+        for m in range(first, len(self.group.hops) + 1):
             self.level(m)
 
     def done(self):
-        net = self.net
-        net.arrived(self.buf.at[net.at((1,))], self.slot["own"])
+        self.net.arrived(self.buf.at[self.group.at((1,))], self.out)
         for k in range(len(self.parts)):
-            for s in subsets(net.turned(k)):
+            for s in subsets(self.group.turned(k)):
                 if s:
-                    net.arrived(self.ref(k, s + (1,)), self.slot[k, s, "core"])
+                    self.net.arrived(self.ref(k, s + (1,)), self.slot[k, s, "core"])
 
     def finish(self):
         self.levels()
@@ -218,135 +241,113 @@
 
 
 class Scatter:
-    def __init__(self, net, part, came, pool):
-        self.net, self.part, self.came = net, part, came
-        self.parts = net.cuts(part.shape[2])
-        self.sets = subsets(net.hops)[::-1]
+    def __init__(self, net, group, part, came, pool):
+        self.net, self.group, self.part, self.came = net, group, part, came
+        self.parts = group.cuts(part.shape[2])
+        self.sets = subsets(group.hops)[::-1]
+        self.count = len(self.sets)
         if (pool, "base") not in net.named:
-            net.named[pool, "base"] = net.slots(len(self.sets))
+            net.named[pool, "base"] = net.slots(self.count)
         self.base = net.named[pool, "base"]
         self.slot = {}
         for k in range(len(self.parts)):
-            for step in range(len(net.hops)):
-                for s in subsets(net.turned(k)[step:]):
-                    if net.turned(k)[step] in s:
+            for step in range(len(group.hops)):
+                for s in subsets(group.turned(k)[step:]):
+                    if group.turned(k)[step] in s:
                         self.slot[k, s] = net.slot(pool, k, s)
-        self.sent = []
-
-    def go(self, *args, **kw):
-        made = self.net.copy(*args, **kw)
-        made.start()
-        self.sent.append(made)
 
     def chip(self, k):
-        net = self.net
-        count = len(net.hops)
-        index = 0
-        turn = len(self.sets) - 1 - k
-        for j, hop in enumerate(net.hops):
-            far = (turn // (2 ** (count - 1 - j))) % 2
-            index = index + hop * (((net.c // hop) + far) % 2)
-        return index
+        return self.group.chip(self.count - 1 - k)
 
     def sets_of(self, k):
-        net = self.net
-        count = len(net.hops)
-        turn = len(self.sets) - 1 - k
-        return tuple(hop for j, hop in enumerate(net.hops) if (turn // (2 ** (count - 1 - j))) % 2)
-
-    def core_copy(self, k):
-        net = self.net
+        hops = self.group.hops
+        turn = self.count - 1 - k
+        return tuple(hop for j, hop in enumerate(hops) if (turn // (2 ** (len(hops) - 1 - j))) % 2)
+
+    def push(self, k):
         first = self.chip(k)
-        mine = lax.rem(net.c, 2)
-        return net.copy(
-            self.part.at[first + 1 - mine], self.came.at[first + mine], self.base + k, ctx=net.at((1,))
-        )
-
-    def push(self, k):
-        self.core_copy(k).start()
+        mine = lax.rem(self.net.c, 2)
+        self.net.copy(
+            self.part.at[first + 1 - mine], self.came.at[first + mine], self.base + k, out=self.base, **self.group.peer(1)
+        ).start()
 
     def fold(self):
-        net = self.net
-        part, came = self.part, self.came
-        for k in range(len(self.sets)):
+        part, came, at = self.part, self.came, self.group.at
+        for k in range(self.count):
             s = self.sets_of(k)
-            mine = net.at(s)
-            other = net.at(s + (1,))
-            net.arrived(came.at[other], self.base + k)
-            part[mine] = (part[mine].astype(f32) + came[other].astype(f32)).astype(bf)
+            self.net.arrived(came.at[at(s + (1,))], self.base + k)
+            part[at(s)] = (part[at(s)].astype(f32) + came[at(s + (1,))].astype(f32)).astype(bf)
             for p in range(len(self.parts)):
                 self.onward(p, 0, s)
 
     def onward(self, p, step, s):
-        net = self.net
-        order = net.turned(p)
+        order = self.group.turned(p)
         if step < len(order) and order[step] in s:
             key = tuple(h for h in order if h in s)
             rest = tuple(h for h in s if h != order[step])
             cut = self.parts[p]
-            self.go(
-                self.part.at[net.at(s), :, cut],
-                self.came.at[net.at(rest), :, cut],
-                self.slot[p, key],
-                ctx=net.at((order[step],)),
-            )
+            self.net.copy(
+                self.part.at[self.group.at(s), :, cut],
+                self.came.at[self.group.at(rest), :, cut],
+                self.slot[p, key], out=self.base, **self.group.peer(order[step]),
+            ).start()
 
     def reduce(self, result):
-        net = self.net
-        part, came = self.part, self.came
-        count = len(net.hops)
+        part, came, at = self.part, self.came, self.group.at
+        count = len(self.group.hops)
         for step in range(count):
             for p in range(len(self.parts)):
-                order = net.turned(p)
+                order = self.group.turned(p)
                 cut = self.parts[p]
                 for s in subsets(order[step + 1:])[::-1]:
                     far = s + (order[step],)
                     key = tuple(h for h in order if h in far)
-                    net.arrived(came.at[net.at(far), :, cut], self.slot[p, key])
-                    total = part[net.at(s), :, cut].astype(f32) + came[net.at(far), :, cut].astype(f32)
+                    self.net.arrived(came.at[at(far), :, cut], self.slot[p, key])
+                    total = part[at(s), :, cut].astype(f32) + came[at(far), :, cut].astype(f32)
                     if step == count - 1:
                         result(cut, total)
                     else:
-                        part[net.at(s), :, cut] = total.astype(bf)
+                        part[at(s), :, cut] = total.astype(bf)
                         self.onward(p, step + 1, s)
         if not count:
-            result(slice(None), part[net.c].astype(f32))
+            result(slice(None), part[self.group.own].astype(f32))
 
     def drain(self):
-        for k in range(len(self.sets)):
-            self.core_copy(k).wait_send()
-        for made in self.sent:
-            made.wait_send()
-        self.sent = []
-
-
-def count_slots(n, nz):
+        ref = self.part.at[pl.ds(0, self.group.blocks - 1)]
+        self.net.copy(ref, ref, self.base, out=self.base).wait_send()
+
+
+def count_slots(n, nz, q):
     hops = n.bit_length() - 2
-    trees = 1 + max(1, hops) * 2 * (2**hops - 1)
-    sums = 2**hops + max(1, hops) * (2**hops - 1)
-    return 2 * trees + 2 * sums + 12 * (nz - 1) + 6 * (n - 1) + n.bit_length() + nz.bit_length() - 2
+    total = 13 * (nz - 1) + 6 + 6 * (n - 1) + n.bit_length() + nz.bit_length() - 2
+    for h in (hops, hops + 1)[:q]:
+        total += 2 * (1 + max(1, h) * 2 * (2**h - 1)) + 2 * (2**h + max(1, h) * (2**h - 1))
+    return total
 
 
 def layer(dims, *refs):
-    (n, nz, t, te, w, fw, hpd) = dims
+    (n, nz, q, t, te, w, fw, hpd) = dims
     (x_ref, e_ref, g_ref, segd_ref, segs_ref, wsl_ref, up_ref, down_ref, vec_ref,
      mixed_ref, gtok_ref, genc_ref, fu, fd, fas, fac, fos, foc, vt, hold1, hold2,
-     n1x, ex, n2f, wbuf, wo, wup, wdown,
+     n1x, ex, gbuf, nbuf, wbuf, wo, wup, wdown,
      qa1, ka1, v1, vt1, ot1, ob1, lse1, qa2, ka2, v2, vt2, ot2, ob2, lse2,
      x1, x2, pa, ra, pm, rm, dy2f,
      act, du, gu, gd, gas, gac, gos, goc, ru, rd, ras, rac, ros, roc,
-     vcame, dlt, dqacc, bias_ref, bup_ref,
+     su, sd, vcame, dlt, dqacc, bias_ref, bup_ref,
      send, recv, local) = refs
     length, lenc = n * t, n * te
+    rows_wide = q * length
     share = D // (n * nz)
     dz = D // nz
     nq, nk2 = length // TILE, lenc // TILE
     nbt, nbe = TILE // t, TILE // te
-    net = Net(n, nz, send, recv)
-    c, z = net.c, net.z
+    net = Net(n, nz, q, send, recv)
+    plane, wide_group = net.plane, net.wide
+    c, z, parity = net.c, net.z, net.parity
     lane = lax.broadcasted_iota(jnp.int32, (1, LANES), 1)
 
-    dqkv, dq2, dkv2 = act.at[:, pl.ds(0, 384)], act.at[:, pl.ds(0, LANES)], act.at[pl.ds(0, lenc), pl.ds(LANES, 256)]
+    rows1 = pl.ds(0, length)
+    dqkv, dq2, dkv2 = act.at[rows1, pl.ds(0, 384)], act.at[rows1, pl.ds(0, LANES)], act.at[pl.ds(0, lenc), pl.ds(LANES, 256)]
     dom = [du.at[:, pl.ds(h * LANES, LANES)] for h in range(hpd)]
     dx = gtok_ref
 
@@ -364,7 +365,9 @@
         return store
 
     zrows = pl.ds(pl.multiple_of(z * dz, dz), dz)
-    fcols = pl.ds(pl.multiple_of(c * fw, LANES), fw)
+
+    def feed_cols(zz):
+        return pl.ds(pl.multiple_of((lax.rem(zz, q) * n + c) * fw, LANES), fw)
 
     def local_copy(src, dst, k):
         made = pltpu.make_async_copy(src, dst, local.at[k])
@@ -381,44 +384,80 @@
     else:
         own_cols = [local_copy(wsl_ref, wbuf.at[zrows, :], 0)]
     own_feed = [
-        local_copy(up_ref.at[:, fcols], wup.at[zrows, :], 8),
-        local_copy(down_ref.at[:, fcols], wdown.at[zrows, :], 9),
+        local_copy(up_ref.at[:, feed_cols(z)], wup.at[zrows, :], 8),
+        local_copy(down_ref.at[:, feed_cols(z)], wdown.at[zrows, :], 9),
     ]
+    hat, _ = normed(x_ref[...].astype(f32))
+    n1x[c, :, pl.ds(0, D)] = (hat * row(0) + row(1)).astype(bf)
+
+    def hot(seg, rows):
+        place = lax.broadcasted_iota(jnp.int32, (LANES, rows), 0) % HD
+        return jnp.where(place == seg[...], 1.0, 0.0).T.astype(bf)
+
+    n1x[c, :, pl.ds(D, LANES)] = hot(segd_ref, t)
     net.greet()
 
-    groups = ((0, 384), (384, 256), (640, 256), (896, 128))
+    groups = ((0, 384), (384, 128), (512, 512))
     wslots = [net.slots(nz - 1) - 1 for _ in groups]
-    upslot, downslot = net.slots(nz - 1) - 1, net.slots(nz - 1) - 1
-    def push_z(src, dst, slot):
+    fslots = [net.slots(nz - 1) - 1 for _ in range(4)]
+
+    ends = jnp.logical_or(z == 0, z == nz - 1)
+    inner = jnp.logical_or(z == 1, z == nz - 2)
+    far_end = jnp.where(z <= 1, nz - 1, 0)
+    near_end = jnp.where(z <= 1, 0, nz - 1)
+    relayed = nz >= 4
+
+    def push_z(src_of, dst, slot, relay):
         for d in range(1, nz):
-            net.go(src, dst, slot + d, fsdp=lax.rem(z + d, nz))
-
-    def await_z(dst_of, slot):
+            peer = lax.rem(z + d, nz)
+            straight = None
+            if relay and d in (1, nz - 1):
+                straight = z != (nz - 1 if d == 1 else 0)
+            net.go(src_of(peer), dst, slot + d, fsdp=peer, when=straight)
+
+    def relay_z(rows_of, slot):
+        rows = rows_of(far_end)
+        came = slot + lax.rem(z + nz - far_end, nz)
+
+        @pl.when(inner)
+        def _():
+            net.arrived(rows, came)
+
+        net.go(rows, rows, slot + jnp.where(z <= 1, 1, nz - 1), out=net.extra(), fsdp=near_end, when=inner)
+
+    def await_z(rows_of, slot, relay):
         for d in range(1, nz):
-            net.arrived(dst_of(lax.rem(z + nz - d, nz)), slot + d)
+            source = lax.rem(z + nz - d, nz)
+            if not relay:
+                net.arrived(rows_of(source), slot + d)
+                continue
+
+            @pl.when(jnp.logical_not(jnp.logical_and(inner, source == far_end)))
+            def _():
+                net.arrived(rows_of(source), slot + d)
 
     def weight_rows(zz, k):
         first, size = groups[k]
         return wbuf.at[pl.ds(pl.multiple_of(zz * dz, dz), dz), pl.ds(first, size)]
 
     def push_weights(k):
-        first, size = groups[k]
-        push_z(weight_rows(z, k), weight_rows(z, k), wslots[k])
-
+        push_z(lambda peer: weight_rows(z, k), weight_rows(z, k), wslots[k], relayed and k == 2)
+
+    half = dz // 2
+
+    def feed_rows(k):
+        buf = (wup, wdown)[k // 2]
+        return lambda zz: buf.at[pl.ds(pl.multiple_of(zz * dz + (k % 2) * half, half), half), :]
+
+    def push_feed(k):
+        ref = (up_ref, down_ref)[k // 2]
+        push_z(lambda peer: ref.at[pl.ds((k % 2) * half, half), feed_cols(peer)], feed_rows(k)(z), fslots[k], relayed and k < 3)
+
+    gat1 = Gather(net, plane, n1x, "main")
+    gat1.start()
     for made in own_cols:
         made.wait()
     push_weights(0)
-
-    hat, _ = normed(x_ref[...].astype(f32))
-    n1x[c, :, pl.ds(0, D)] = (hat * row(0) + row(1)).astype(bf)
-
-    def hot(seg, rows):
-        place = lax.broadcasted_iota(jnp.int32, (LANES, rows), 0) % HD
-        return jnp.where(place == seg[...], 1.0, 0.0).T.astype(bf)
-
-    n1x[c, :, pl.ds(D, LANES)] = hot(segd_ref, t)
-    gat1 = Gather(net, n1x, "main")
-    gat1.start()
     ex[c, :, pl.ds(0, D)] = e_ref[...]
     ex[c, :, pl.ds(D, LANES)] = hot(segs_ref, te)
     for k in range(1, len(groups)):
@@ -431,16 +470,22 @@
             own = jnp.where(c == cc, vec_ref[line:line + 1, cc * w:(cc + 1) * w], own)
         bias_ref[k:k + 1, 0:w] = own
     own = vec_ref[13:14, 0:fw]
-    for cc in range(1, n):
+    for cc in range(1, n * q):
         line, first = 13 + cc * fw // D, cc * fw % D
-        own = jnp.where(c == cc, vec_ref[line:line + 1, first:first + fw], own)
+        own = jnp.where(wide_group.own == cc, vec_ref[line:line + 1, first:first + fw], own)
     bup_ref[0:1, :] = own
     vt[8:9, :] = jnp.sum(g_ref[...].astype(f32), axis=0, keepdims=True)
+    if relayed:
+        @pl.when(ends)
+        def _():
+            for came in (ru, rd, rac, roc):
+                came[far_end] = jnp.zeros(came.shape[1:], bf)
+
     gat1.levels()
-    gate = Gather(net, ex, "side")
+    gate = Gather(net, plane, ex, "side")
     gate.start()
     gat1.done()
-    await_z(lambda zz: weight_rows(zz, 0), wslots[0])
+    await_z(lambda zz: weight_rows(zz, 0), wslots[0], False)
 
     def tile_of(buf, i, per, columns):
         return buf[pl.ds(i * per, per), :, columns].reshape(TILE, columns.size)
@@ -477,12 +522,16 @@
 
     lax.fori_loop(0, nq, qkv_tile, 0)
 
-    gf, n3f, dy1f = n1x.at[:, :, pl.ds(0, D)], n2f, n2f
-
-    away1 = local_copy(gf, hold1, 10)
-
-    push_z(up_ref.at[:, fcols], wup.at[zrows, :], upslot)
-    push_z(down_ref.at[:, fcols], wdown.at[zrows, :], downslot)
+    n1f, n3f = n1x.at[:, :, pl.ds(0, D)], nbuf
+    n2f = dy1f = nbuf.at[pl.ds(parity * n, n)] if q == 2 else nbuf
+    gf = gbuf if q == 2 else n1f
+    n2back = gf.at[pl.ds(0, n)]
+
+    if q == 1:
+        away1 = local_copy(n1f, hold1, 10)
+
+    push_feed(0)
+    push_feed(1)
 
     def attend(qa, ka, vt_ref, ot, ob, lse, keys, causal):
         def one(j, _):
@@ -525,20 +574,19 @@
             ot[...] = jnp.zeros_like(ot)
         lax.fori_loop(0, nq, one, 0)
 
-    attend(qa1, ka1, vt1, ot1, ob1, lse1, nq, True)
-
-    await_z(lambda zz: weight_rows(zz, 1), wslots[1])
-    await_z(lambda zz: weight_rows(zz, 2), wslots[2])
+    await_z(lambda zz: weight_rows(zz, 1), wslots[1], False)
     oslots = [net.slots(n - 1) - 1, net.slots(n - 1) - 1]
 
     def out_rows(j, cc):
-        return wbuf.at[pl.ds(pl.multiple_of(cc * w, w), w), pl.ds(640 + j * LANES, LANES)]
-
-    for j in range(2):
+        return wbuf.at[pl.ds(pl.multiple_of(cc * w, w), w), pl.ds(OUT_AT[j], LANES)]
+
+    def push_out(j):
         for d in range(1, n):
             peer = lax.rem(c + d, n)
             net.go(out_rows(j, peer), wor_of(j, c), oslots[j] + d, ctx=peer)
-        wor_of(j, c)[...] = wbuf[pl.ds(pl.multiple_of(c * w, w), w), pl.ds(640 + j * LANES, LANES)]
+        wor_of(j, c)[...] = wbuf[pl.ds(pl.multiple_of(c * w, w), w), pl.ds(OUT_AT[j], LANES)]
+
+    push_out(0)
 
     def await_out(j):
         for d in range(1, n):
@@ -548,7 +596,10 @@
         wo[j, pl.ds(0, w), :] = jnp.concatenate(
             [pm[cc, pl.ds(0, w), pl.ds(j * LANES, LANES)][:, :w] for cc in range(n)], axis=-1)
 
-    gate.finish()
+    gate.levels()
+    attend(qa1, ka1, vt1, ot1, ob1, lse1, nq, True)
+
+    gate.done()
     await_out(0)
 
     def partial(scat, rows_of, weight_of, per):
@@ -558,39 +609,44 @@
             scat.push(k)
             return _
 
-        lax.fori_loop(0, n // 2, one, 0)
+        lax.fori_loop(0, scat.count, one, 0)
 
     def flat(buf, per):
         return lambda first: buf[pl.ds(pl.multiple_of(first * per, 2 * per), 2 * per), :]
 
-    rs1 = Scatter(net, pa, ra, "sum")
+    rs1 = Scatter(net, plane, pa.at[pl.ds(0, n)], ra.at[pl.ds(0, n)], "sum")
     partial(rs1, flat(ob1, t), lambda rows: dot(rows, wo[0]), t)
 
     def kv2_tile(i, _):
         rows = tile_rows(i)
-        got = dot(tile_of(ex, i, nbe, pl.ds(0, D)), wbuf[:, 384:640])
+        got = dot(tile_of(ex, i, nbe, pl.ds(0, D)), wbuf[:, 512:768])
         oh = tile_of(ex, i, nbe, pl.ds(D, LANES))
         put_k(ka2, got[:, 0:128], oh, rows)
         put_v(v2, vt2, got[:, 128:256] + bias_ref[3:4, :], rows, i)
         return _
 
     rs1.fold()
-    lax.fori_loop(0, nk2, kv2_tile, 0)
+    if relayed:
+        relay_z(lambda zz: weight_rows(zz, 2), wslots[2])
     rs1.reduce(into(x1))
     x1[...] = x_ref[...].astype(f32) + (x1[...] + row(8))
     hat, _ = normed(x1[...])
     n2f[c] = (hat * row(2) + row(3)).astype(bf)
     gat1.drain()
-    away1.wait()
-    gat2 = Gather(net, n2f, "main")
+    if q == 1:
+        away1.wait()
+    gat2 = Gather(net, plane, n2f, "main")
     gat2.start()
     rs1.drain()
     gate.drain()
-    await_out(1)
-    await_z(lambda zz: weight_rows(zz, 3), wslots[3])
-    gat2.finish()
-    gf[c] = g_ref[...]
-    gatg = Gather(net, gf, "side")
+    push_feed(2)
+    push_feed(3)
+    gat2.levels()
+    await_z(lambda zz: weight_rows(zz, 2), wslots[2], relayed)
+    push_out(1)
+    gat2.done()
+    gf[wide_group.own] = g_ref[...]
+    gatg = Gather(net, wide_group, gf, "side" if q == 1 else "wideside")
     gatg.start()
 
     def q2_tile(i, _):
@@ -599,32 +655,39 @@
         return _
 
     lax.fori_loop(0, nq, q2_tile, 0)
+    lax.fori_loop(0, nk2, kv2_tile, 0)
+    if relayed:
+        relay_z(feed_rows(0), fslots[0])
     away2 = local_copy(n2f, hold2, 11)
     gatg.level(1)
     attend(qa2, ka2, vt2, ot2, ob2, lse2, nk2, False)
     away2.wait()
     gat2.drain()
-    rs2 = Scatter(net, pa, ra, "sum")
+    await_out(1)
+    rs2 = Scatter(net, plane, pa.at[pl.ds(0, n)], ra.at[pl.ds(0, n)], "sum")
     partial(rs2, flat(ob2, t), lambda rows: dot(rows, wo[1]), t)
-    for m in range(2, len(net.hops) + 1):
-        gatg.level(m)
+    gatg.levels(2)
     rs2.fold()
+    if relayed:
+        relay_z(feed_rows(1), fslots[1])
     rs2.reduce(into(x2))
     x2[...] = x1[...] + (x2[...] + row(11))
     hat, _ = normed(x2[...])
-    n3f[c] = (hat * row(4) + row(5)).astype(bf)
-    gat3 = Gather(net, n3f, "main")
+    n3f[wide_group.own] = (hat * row(4) + row(5)).astype(bf)
+    gat3 = Gather(net, wide_group, n3f, "main" if q == 1 else "wide")
     gat3.start()
     rs2.drain()
     gatg.done()
     for made in own_feed:
         made.wait()
     gat3.finish()
-    await_z(lambda zz: wup.at[pl.ds(pl.multiple_of(zz * dz, dz), dz), :], upslot)
-    await_z(lambda zz: wdown.at[pl.ds(pl.multiple_of(zz * dz, dz), dz), :], downslot)
-
-    rs3 = Scatter(net, pa, ra, "sum")
-    rsm = Scatter(net, pm, rm, "sum2")
+    if relayed:
+        relay_z(feed_rows(2), fslots[2])
+    for k in range(4):
+        await_z(feed_rows(k), fslots[k], relayed and k < 3)
+
+    rs3 = Scatter(net, wide_group, pa, ra, "sum" if q == 1 else "widesum")
+    rsm = Scatter(net, wide_group, pm, rm, "sum2" if q == 1 else "widesum2")
     fc = min(fw, 512)
 
     def feed_tile(k, sums):
@@ -645,12 +708,12 @@
         rs3.push(k)
         return tuple(out)
 
-    sums = lax.fori_loop(0, n // 2, feed_tile, tuple(jnp.zeros((1, fc), f32) for _ in range(fw // fc)))
+    sums = lax.fori_loop(0, rs3.count, feed_tile, tuple(jnp.zeros((1, fc), f32) for _ in range(fw // fc)))
     for f in range(fw // fc):
-        for cc in range(n):
+        for cc in range(n * q):
             place = cc * fw + f * fc
             line = 9 + 4 * wide + place // D
-            vt[line:line + 1, pl.ds(place % D, fc)] = jnp.where(c == cc, sums[f], 0.0)
+            vt[line:line + 1, pl.ds(place % D, fc)] = jnp.where(wide_group.own == cc, sums[f], 0.0)
     rs3.fold()
     partial(rsm, flat(act, t), lambda rows: dot_t(rows, wdown[...]), t)
     rsm.fold()
@@ -669,22 +732,50 @@
     def whole(buf, rows):
         return lambda cols: buf[:, :, cols].reshape(rows, TILE)
 
-    zslots = [net.slots(nz - 1) - 1 for _ in range(6)]
+    zslots = [net.slots(nz) - 1 for _ in range(6)]
+    last = (4, 5)
 
     def push_grad(mine, came, k):
         for d in range(1, nz):
             peer = lax.rem(z + d, nz)
-            net.go(mine.at[peer], came.at[z], zslots[k] + d, fsdp=peer)
+            when = None
+            if relayed and k not in last:
+                when = jnp.logical_not(jnp.logical_and(
+                    jnp.logical_or(ends, inner), peer == far_end))
+            net.go(mine.at[peer], came.at[z], zslots[k] + d, fsdp=peer, when=when)
+        if relayed and k not in last:
+            step = jnp.where(z == 0, 1, nz - 2)
+            net.go(mine.at[far_end], came.at[step], zslots[k] + nz, out=net.extra(), fsdp=step, when=ends)
+
+    def relay_grad(mine, came, k):
+        if not relayed:
+            return
+
+        @pl.when(inner)
+        def _():
+            net.arrived(came.at[z], zslots[k] + nz)
+            mine[far_end] = (mine[far_end].astype(f32) + came[z].astype(f32)).astype(bf)
+
+        net.go(mine.at[far_end], came.at[z], zslots[k] + lax.rem(far_end - z + nz, nz), out=net.extra(), fsdp=far_end,
+               when=inner)
+
+    def grad_arrived(came, k, d):
+        peer = lax.rem(z + nz - d, nz)
+        if relayed and k not in last and d in (1, nz - 1):
+            @pl.when(z != (0 if d == 1 else nz - 1))
+            def _():
+                net.arrived(came.at[peer], zslots[k] + d)
+        else:
+            net.arrived(came.at[peer], zslots[k] + d)
+        return came[peer].astype(f32)
 
     def sum_grad(mine, came, k):
         total = mine[z].astype(f32)
         for d in range(1, nz):
-            peer = lax.rem(z + nz - d, nz)
-            net.arrived(came.at[peer], zslots[k] + d)
-            total = total + came[peer].astype(f32)
+            total = total + grad_arrived(came, k, d)
         return total.astype(bf)
 
-    weight_grad(whole(n3f, length), lambda: du[...], gu, pl.ds(0, fw))
+    weight_grad(whole(n3f, rows_wide), lambda: du[...], gu, pl.ds(0, fw))
     push_grad(gu, ru, 0)
     gat3.drain()
     gatg.drain()
@@ -695,20 +786,16 @@
     dx[...] = g_ref[...].astype(f32) + back
     dy = dx[...].astype(bf)
     dy2f[c] = dy
-    gat4 = Gather(net, dy2f, "main")
+    gat4 = Gather(net, plane, dy2f, "main")
     gat4.start()
     vt[7:8, :] = jnp.sum(dy.astype(f32), axis=0, keepdims=True)
     rs3.drain()
     gat4.levels()
-    weight_grad(whole(gf, length), lambda: act[...], gd, pl.ds(0, fw))
+    weight_grad(whole(gf, rows_wide), lambda: act[...], gd, pl.ds(0, fw))
     push_grad(gd, rd, 1)
-    back2 = local_copy(hold2, gf, 12)
-
-    def store_mixed(cut, total):
-        mixed_ref[:, cut] = (x2[:, cut] + (total + vec_ref[12:13, cut])).astype(bf)
-
-    rsm.reduce(store_mixed)
+    back2 = local_copy(hold2, n2back, 12)
     gat4.done()
+    relay_grad(gu, ru, 0)
 
     def attend_back(qa, ka, v, ot, lse, dyf, out_w, keys, causal, dq_ref, dq_cols, dkv_ref, dk_cols, dv_cols):
         def grads(i, _):
@@ -777,15 +864,21 @@
 
     first3 = [pl.ds(k * LANES, LANES) for k in range(3)]
     attend_back(qa2, ka2, v2, ot2, lse2, dy2f, wo.at[1], nk2, False, dq2, first3[0], dkv2, first3[0], first3[1])
-    rs4 = Scatter(net, pa, ra, "sum")
+    rs4 = Scatter(net, plane, pa.at[pl.ds(0, n)], ra.at[pl.ds(0, n)], "sum")
     partial(rs4, flat(dq2, t), lambda rows: dot_t(rows, wbuf[:, 896:1024]), t)
+    def store_mixed(cut, total):
+        mixed_ref[:, cut] = (x2[:, cut] + (total + vec_ref[12:13, cut])).astype(bf)
+
+    rsm.reduce(store_mixed)
     rs4.fold()
 
     weight_grad(whole(ex, lenc), lambda: dkv2[...], gac, pl.ds(0, 256))
     back2.wait()
-    weight_grad(whole(gf, length), lambda: dq2[...], gac, pl.ds(256, 128))
-    back1 = local_copy(hold1, gf, 13)
+    weight_grad(whole(n2back, length), lambda: dq2[...], gac, pl.ds(256, 128))
+    if q == 1:
+        back1 = local_copy(hold1, n1f, 13)
     push_grad(gac, rac, 2)
+    relay_grad(gd, rd, 1)
 
     def out_grad(ob, dyf, out):
         for cut in (0, 1):
@@ -802,30 +895,33 @@
     dy = dx[...].astype(bf)
     dy1f[c] = dy
     gat4.drain()
-    gat5 = Gather(net, dy1f, "main")
+    gat5 = Gather(net, plane, dy1f, "main")
     gat5.start()
     vt[6:7, :] = jnp.sum(dy.astype(f32), axis=0, keepdims=True)
     head_sum(2, dq2, first3[0])
     head_sum(3, dkv2, first3[1])
     rs4.drain()
     rsm.drain()
-    rse = Scatter(net, pm.at[:, pl.ds(0, te), :], rm.at[:, pl.ds(0, te), :], "sum2")
-    partial(rse, flat(dkv2, te), lambda rows: dot_t(rows, wbuf[:, 384:640]), te)
+    rse = Scatter(net, plane, pm.at[pl.ds(0, n), pl.ds(0, te), :], rm.at[pl.ds(0, n), pl.ds(0, te), :], "sum2")
+    partial(rse, flat(dkv2, te), lambda rows: dot_t(rows, wbuf[:, 512:768]), te)
     gat5.levels()
     rse.fold()
     out_grad(ob2, dy2f, goc)
     push_grad(goc, roc, 3)
-    rse.reduce(into(genc_ref))
     gat5.done()
+    relay_grad(gac, rac, 2)
+    out_grad(ob1, dy1f, gos)
+    push_grad(gos, ros, 5)
     attend_back(qa1, ka1, v1, ot1, lse1, dy1f, wo.at[0], nq, True, dqkv, first3[0], dqkv, first3[1], first3[2])
-    rs5 = Scatter(net, pa, ra, "sum")
+    rs5 = Scatter(net, plane, pa.at[pl.ds(0, n)], ra.at[pl.ds(0, n)], "sum")
     partial(rs5, flat(dqkv, t), lambda rows: dot_t(rows, wbuf[:, 0:384]), t)
     rs5.fold()
-    back1.wait()
-    weight_grad(whole(gf, length), lambda: dqkv[...], gas, pl.ds(0, 384))
+    rse.reduce(into(genc_ref))
+    if q == 1:
+        back1.wait()
+    weight_grad(whole(n1f, length), lambda: dqkv[...], gas, pl.ds(0, 384))
     push_grad(gas, ras, 4)
-    out_grad(ob1, dy1f, gos)
-    push_grad(gos, ros, 5)
+    relay_grad(goc, roc, 3)
     rs5.reduce(into(x2))
     back, gain_g, shift_g = norm_back(x_ref[...].astype(f32), row(0), x2[...])
     vt[0:1, :] = gain_g
@@ -835,7 +931,7 @@
     head_sum(1, dqkv, first3[2])
 
     vslots = net.slots(vcame.shape[0])
-    pairs = [("ctx", b) for b in net.hops + [1]] + [("fsdp", 1 << k) for k in range(nz.bit_length() - 1)]
+    pairs = [("ctx", b) for b in plane.hops + [1]] + [("fsdp", 1 << k) for k in range(nz.bit_length() - 1)]
 
     def swap(k):
         axis, b = pairs[k]
@@ -850,13 +946,26 @@
         net.arrived(vcame.at[k], vslots + k)
         vt[...] = vt[...] + vcame[k]
 
-    def exchange(mine, came, k, out):
+    def sum_feed(mine, came, k, total):
+        for r in range(q):
+            got = 0.0
+            for d in range(r, nz, q):
+                if d == 0:
+                    got = got + mine[z].astype(f32)
+                else:
+                    got = got + grad_arrived(came, k, d)
+            total[:, lax.rem(parity + q - r, q)] = got.astype(bf)
+
+    def sum_heads(mine, came, k):
+        mine[z] = sum_grad(mine, came, k)
+        return mine.at[z]
+
+    def exchange(total, out):
         slot = net.slots(n - 1) - 1
-        mine[z] = sum_grad(mine, came, k)
-        out[c] = mine[z, c]
+        out[c] = total[c]
         for d in range(1, n):
             peer = lax.rem(c + d, n)
-            net.go(mine.at[z, peer], out.at[c], slot + d, ctx=peer)
+            net.go(total.at[peer], out.at[c], slot + d, ctx=peer)
 
         def done():
             for d in range(1, n):
@@ -865,9 +974,9 @@
 
     waits = []
     todo = [
-        lambda: waits.append(exchange(gu, ru, 0, fu)),
-        lambda: waits.append(exchange(gd, rd, 1, fd)),
-        lambda: waits.append(exchange(gac, rac, 2, fac)),
+        lambda: (sum_feed(gu, ru, 0, su), waits.append(exchange(su, fu))),
+        lambda: (sum_feed(gd, rd, 1, sd), waits.append(exchange(sd, fd))),
+        lambda: waits.append(exchange(sum_heads(gac, rac, 2), fac)),
     ]
     for k in range(len(pairs)):
         made = swap(k)
@@ -877,7 +986,7 @@
     for step in todo:
         step()
     foc[...] = sum_grad(goc, roc, 3)
-    waits.append(exchange(gas, ras, 4, fas))
+    waits.append(exchange(sum_heads(gas, ras, 4), fas))
     fos[...] = sum_grad(gos, ros, 5)
     for wait in waits:
         wait()
@@ -885,7 +994,7 @@
     rse.drain()
     gat5.drain()
     net.drain()
-    assert net.used == count_slots(n, nz)
+    assert net.used == count_slots(n, nz, q) and net.extras <= EXTRAS
 
 
 def body(tokens, encoder, dec_seg, src_seg, attn_w, up_w, down_w, vec, cot):
@@ -893,7 +1002,8 @@
     c = lax.axis_index("ctx")
     t, te = tokens.shape[1], encoder.shape[1]
     ff = up_w.shape[1]
-    w, fw = D // n, ff // n
+    q = 1
+    w, fw = D // n, ff // (n * q)
     hpd = w // HD
     dz = D // nz
     share = D // (n * nz)
@@ -905,8 +1015,8 @@
         attn_w = jnp.pad(wsl, ((0, 0), (0, 0), (0, LANES - w))).reshape(dz, 8 * LANES)
 
     nq, nk2 = length // TILE, lenc // TILE
-    slots = count_slots(n, nz)
-    dims = (n, nz, t, te, w, fw, hpd)
+    slots = count_slots(n, nz, q)
+    dims = (n, nz, q, t, te, w, fw, hpd)
     wide = -(-n * LANES // D)
     vrows = -(-(9 + 4 * wide + ff // D) // 8) * 8
     steps = n.bit_length() + nz.bit_length() - 2
@@ -914,8 +1024,8 @@
         jax.ShapeDtypeStruct((t, D), bf),
         jax.ShapeDtypeStruct((t, D), f32),
         jax.ShapeDtypeStruct((te, D), f32),
-        jax.ShapeDtypeStruct((n, share, fw), bf),
-        jax.ShapeDtypeStruct((n, share, fw), bf),
+        jax.ShapeDtypeStruct((n, q, share, fw), bf),
+        jax.ShapeDtypeStruct((n, q, share, fw), bf),
         jax.ShapeDtypeStruct((n, share, 384), bf),
         jax.ShapeDtypeStruct((n, share, 384), bf),
         jax.ShapeDtypeStruct((share, D), bf),
@@ -933,14 +1043,14 @@
         ]
 
     scratch = [
-        pltpu.VMEM((n, t, D + LANES), bf), pltpu.VMEM((n, te, D + LANES), bf), pltpu.VMEM((n, t, D), bf),
+        pltpu.VMEM((n, t, D + LANES), bf), pltpu.VMEM((n, te, D + LANES), bf),
+        pltpu.VMEM((q * n, t, D) if q == 2 else (1, 16, LANES), bf), pltpu.VMEM((q * n, t, D), bf),
         pltpu.VMEM((D, 8 * LANES), bf), pltpu.VMEM((2, LANES, D), bf),
         pltpu.VMEM((D, fw), bf), pltpu.VMEM((D, fw), bf),
         *attn_scratch(length), *attn_scratch(lenc),
         pltpu.VMEM((t, D), f32), pltpu.VMEM((t, D), f32),
-        pltpu.VMEM((n, t, D), bf), pltpu.VMEM((n, t, D), bf), pltpu.VMEM((n, t, D), bf), pltpu.VMEM((n, t, D), bf),
-        pltpu.VMEM((n, t, D), bf),
-        pltpu.VMEM((length, fw), bf), pltpu.VMEM((length, fw), bf),
+        *[pltpu.VMEM((q * n, t, D), bf) for _ in range(4)], pltpu.VMEM((n, t, D), bf),
+        pltpu.VMEM((q * length, fw), bf), pltpu.VMEM((q * length, fw), bf),
     ]
     for _ in range(2):
         scratch += [
@@ -949,10 +1059,10 @@
             pltpu.VMEM((nz, share, D), bf), pltpu.VMEM((nz, share, D), bf),
         ]
     scratch += [
-        pltpu.VMEM((steps, vrows, D), f32),
+        pltpu.VMEM((n, q, share, fw), bf), pltpu.VMEM((n, q, share, fw), bf), pltpu.VMEM((steps, vrows, D), f32),
         pltpu.VMEM((nq, 8, TILE), f32), pltpu.VMEM((length, LANES), f32),
         pltpu.VMEM((8, LANES), f32), pltpu.VMEM((8, fw), f32),
-        pltpu.SemaphoreType.DMA((slots,)), pltpu.SemaphoreType.DMA((slots,)), pltpu.SemaphoreType.DMA((16,)),
+        pltpu.SemaphoreType.DMA((slots + EXTRAS,)), pltpu.SemaphoreType.DMA((slots,)), pltpu.SemaphoreType.DMA((16,)),
     ]
     vmem = pl.BlockSpec(memory_space=pltpu.VMEM)
     hbm = pl.BlockSpec(memory_space=pl.ANY)
@@ -970,7 +1080,7 @@
     )(tokens[0], encoder[0], cot[0], dec_seg, src_seg, attn_w, up_w, down_w, vec)
 
     return pl.pallas_call(
-        functools.partial(closing, (n, w, fw, wide)),
+        functools.partial(closing, (n, q, w, fw, wide)),
         out_shape=(
             jax.ShapeDtypeStruct((1, t, D), bf), jax.ShapeDtypeStruct((1, t, D), f32),
             jax.ShapeDtypeStruct((1, te, D), f32), jax.ShapeDtypeStruct((share, 8 * D), f32),
@@ -989,7 +1099,7 @@
 
 
 def closing(dims, *refs):
-    n, w, fw, wide = dims
+    n, q, w, fw, wide = dims
     given, outs, kept, made, sems = refs[:10], refs[10:17], refs[17:27], refs[27:31], refs[31]
     coming = [pltpu.make_async_copy(given[k], kept[k], sems.at[k]) for k in range(10)]
     straight = [pltpu.make_async_copy(kept[k], outs[k].at[0], sems.at[10 + k]) for k in range(3)]
@@ -1003,12 +1113,12 @@
     fu, fd, fas, fac, fos, foc, vsum = kept
     o_attn, o_up, o_down, o_vec = made
     coming[0].wait()
-    for cc in range(n):
-        o_up[:, pl.ds(cc * fw, fw)] = fu[cc].astype(f32)
+    for cc in range(n * q):
+        o_up[:, pl.ds(cc * fw, fw)] = fu[cc % n, cc // n].astype(f32)
     going[1].start()
     coming[1].wait()
-    for cc in range(n):
-        o_down[:, pl.ds(cc * fw, fw)] = fd[cc].astype(f32)
+    for cc in range(n * q):
+        o_down[:, pl.ds(cc * fw, fw)] = fd[cc % n, cc // n].astype(f32)
     going[2].start()
     for k in range(2, 7):
         coming[k].wait()

time: 317 us -> 299 us (0.943)
  Pallas kernels: 315 us -> 294 us
    pallas_call x1, Pallas kernels: 312 us -> 291 us  [body(): pl.pallas_call(functools.partial(layer, dims), out_shape=out_shape, in_sp...]
where the time goes in v3:
time: 299 us; the launch traced here: 295 us
  Pallas kernels  294 us (98%)
    pallas_call x1, Pallas kernels, body(): pl.pallas_call(functools.partial(layer, dims), out_shape=out_shape, in_sp...  291 us

profile of v3, /device:TPU:8, one launch (start us, length us, event | category | flops | bytes accessed | tf_op | source)
XLA Modules:
  0.0 295.1 jit_solution(6101707028264073300)
XLA Ops:
  0.6 291.0 %layer.1 = (bf16[128,1024]{1,0:T(8,128)(2,1)}, f32[128,1024]{1,0:T(8,128)}, f32[64,1024]{1,0:T(8,128)}, bf16[8,1,32,1024]{3,2,1,0:T(8,128)(2,1)}, bf16[8,1,32,10...) custom-call(bf16[128,1024]{1,0:T(8,128)(2,1)} %bitcast.3, ...), custom_call_target="tpu_custom_call" | custom-call | flops 20999999488 | bytes 30000000 | tf_op jit(solution)/shard_map/layer/pallas_call | solution.py:1069
  291.7 3.3 %closing.1 = (bf16[1,128,1024]{2,1,0:T(8,128)(2,1)}, f32[1,128,1024]{2,1,0:T(8,128)}, f32[1,64,1024]{2,1,0:T(8,128)}, f32[32,8192]{1,0:T(8,128)}, f32[32,8192]{1...) custom-call(bf16[128,1024]{1,0:T(8,128)(2,1)} %get-tuple-element.17.refs_0_, f32[128,1024]{1,0:T(8,128)} %get-tuple-element.18.refs_1_, ...), custom_call_target="tpu_custom_call" | custom-call | tf_op jit(solution)/shard_map/closing/pallas_call | solution.py:1082

commit v4 on v3

--- a/solution.py
+++ b/solution.py
@@ -441,7 +441,7 @@
         return wbuf.at[pl.ds(pl.multiple_of(zz * dz, dz), dz), pl.ds(first, size)]
 
     def push_weights(k):
-        push_z(lambda peer: weight_rows(z, k), weight_rows(z, k), wslots[k], relayed and k == 2)
+        push_z(lambda peer: weight_rows(z, k), weight_rows(z, k), wslots[k], relayed and k != 1)
 
     half = dz // 2
 
@@ -485,7 +485,9 @@
     gate = Gather(net, plane, ex, "side")
     gate.start()
     gat1.done()
-    await_z(lambda zz: weight_rows(zz, 0), wslots[0], False)
+    if relayed:
+        relay_z(lambda zz: weight_rows(zz, 0), wslots[0])
+    await_z(lambda zz: weight_rows(zz, 0), wslots[0], relayed)
 
     def tile_of(buf, i, per, columns):
         return buf[pl.ds(i * per, per), :, columns].reshape(TILE, columns.size)
@@ -530,8 +532,8 @@
     if q == 1:
         away1 = local_copy(n1f, hold1, 10)
 
-    push_feed(0)
-    push_feed(1)
+    for k in range(4):
+        push_feed(k)
 
     def attend(qa, ka, vt_ref, ot, ob, lse, keys, causal):
         def one(j, _):
@@ -639,8 +641,6 @@
     gat2.start()
     rs1.drain()
     gate.drain()
-    push_feed(2)
-    push_feed(3)
     gat2.levels()
     await_z(lambda zz: weight_rows(zz, 2), wslots[2], relayed)
     push_out(1)
@@ -681,43 +681,28 @@
     for made in own_feed:
         made.wait()
     gat3.finish()
+    for k in range(2):
+        await_z(feed_rows(k), fslots[k], relayed)
     if relayed:
         relay_z(feed_rows(2), fslots[2])
-    for k in range(4):
-        await_z(feed_rows(k), fslots[k], relayed and k < 3)
 
     rs3 = Scatter(net, wide_group, pa, ra, "sum" if q == 1 else "widesum")
     rsm = Scatter(net, wide_group, pm, rm, "sum2" if q == 1 else "widesum2")
     fc = min(fw, 512)
 
-    def feed_tile(k, sums):
+    def up_tile(k, _):
         first = rs3.chip(k)
         rows = pl.ds(pl.multiple_of(first * t, 2 * t), 2 * t)
         left = n3f[pl.ds(first, 2)].reshape(2 * t, D)
-        grad = gf[pl.ds(first, 2)].reshape(2 * t, D)
-        out = []
         for f in range(fw // fc):
             cols = pl.ds(f * fc, fc)
             u = dot(left, wup[:, cols]) + bup_ref[0:1, cols]
             cdf, slope = gelu_parts(u)
             act[rows, cols] = (u * cdf).astype(bf)
-            low = (dot(grad, wdown[:, cols]) * slope).astype(bf)
-            du[rows, cols] = low
-            out.append(sums[f] + jnp.sum(low.astype(f32), axis=0, keepdims=True))
-        pa[pl.ds(first, 2)] = dot_t(du[rows, :], wup[...]).astype(bf).reshape(2, t, D)
-        rs3.push(k)
-        return tuple(out)
-
-    sums = lax.fori_loop(0, rs3.count, feed_tile, tuple(jnp.zeros((1, fc), f32) for _ in range(fw // fc)))
-    for f in range(fw // fc):
-        for cc in range(n * q):
-            place = cc * fw + f * fc
-            line = 9 + 4 * wide + place // D
-            vt[line:line + 1, pl.ds(place % D, fc)] = jnp.where(wide_group.own == cc, sums[f], 0.0)
-    rs3.fold()
-    partial(rsm, flat(act, t), lambda rows: dot_t(rows, wdown[...]), t)
-    rsm.fold()
-
+            du[rows, cols] = slope.astype(bf)
+        return _
+
+    lax.fori_loop(0, rs3.count, up_tile, 0)
     per = TILE // (share * nz)
 
     def weight_grad(left_of, right, out, columns):
@@ -736,6 +721,9 @@
     last = (4, 5)
 
     def push_grad(mine, came, k):
+        if relayed and k not in last:
+            step = jnp.where(z == 0, 1, nz - 2)
+            net.go(mine.at[far_end], came.at[step], zslots[k] + nz, out=net.extra(), fsdp=step, when=ends)
         for d in range(1, nz):
             peer = lax.rem(z + d, nz)
             when = None
@@ -743,9 +731,6 @@
                 when = jnp.logical_not(jnp.logical_and(
                     jnp.logical_or(ends, inner), peer == far_end))
             net.go(mine.at[peer], came.at[z], zslots[k] + d, fsdp=peer, when=when)
-        if relayed and k not in last:
-            step = jnp.where(z == 0, 1, nz - 2)
-            net.go(mine.at[far_end], came.at[step], zslots[k] + nz, out=net.extra(), fsdp=step, when=ends)
 
     def relay_grad(mine, came, k):
         if not relayed:
@@ -775,8 +760,38 @@
             total = total + grad_arrived(came, k, d)
         return total.astype(bf)
 
+    weight_grad(whole(gf, rows_wide), lambda: act[...], gd, pl.ds(0, fw))
+    for k in range(2, 4):
+        await_z(feed_rows(k), fslots[k], relayed and k < 3)
+
+    push_grad(gd, rd, 1)
+
+    def down_tile(k, sums):
+        first = rs3.chip(k)
+        rows = pl.ds(pl.multiple_of(first * t, 2 * t), 2 * t)
+        grad = gf[pl.ds(first, 2)].reshape(2 * t, D)
+        out = []
+        for f in range(fw // fc):
+            cols = pl.ds(f * fc, fc)
+            low = (dot(grad, wdown[:, cols]) * du[rows, cols].astype(f32)).astype(bf)
+            du[rows, cols] = low
+            out.append(sums[f] + jnp.sum(low.astype(f32), axis=0, keepdims=True))
+        pa[pl.ds(first, 2)] = dot_t(du[rows, :], wup[...]).astype(bf).reshape(2, t, D)
+        rs3.push(k)
+        return tuple(out)
+
+    sums = lax.fori_loop(0, rs3.count, down_tile, tuple(jnp.zeros((1, fc), f32) for _ in range(fw // fc)))
+    for f in range(fw // fc):
+        for cc in range(n * q):
+            place = cc * fw + f * fc
+            line = 9 + 4 * wide + place // D
+            vt[line:line + 1, pl.ds(place % D, fc)] = jnp.where(wide_group.own == cc, sums[f], 0.0)
+    rs3.fold()
     weight_grad(whole(n3f, rows_wide), lambda: du[...], gu, pl.ds(0, fw))
     push_grad(gu, ru, 0)
+    partial(rsm, flat(act, t), lambda rows: dot_t(rows, wdown[...]), t)
+    rsm.fold()
+
     gat3.drain()
     gatg.drain()
     rs3.reduce(into(dx))
@@ -791,11 +806,8 @@
     vt[7:8, :] = jnp.sum(dy.astype(f32), axis=0, keepdims=True)
     rs3.drain()
     gat4.levels()
-    weight_grad(whole(gf, rows_wide), lambda: act[...], gd, pl.ds(0, fw))
-    push_grad(gd, rd, 1)
     back2 = local_copy(hold2, n2back, 12)
     gat4.done()
-    relay_grad(gu, ru, 0)
 
     def attend_back(qa, ka, v, ot, lse, dyf, out_w, keys, causal, dq_ref, dq_cols, dkv_ref, dk_cols, dv_cols):
         def grads(i, _):
@@ -871,6 +883,7 @@
 
     rsm.reduce(store_mixed)
     rs4.fold()
+    relay_grad(gd, rd, 1)
 
     weight_grad(whole(ex, lenc), lambda: dkv2[...], gac, pl.ds(0, 256))
     back2.wait()
@@ -878,7 +891,6 @@
     if q == 1:
         back1 = local_copy(hold1, n1f, 13)
     push_grad(gac, rac, 2)
-    relay_grad(gd, rd, 1)
 
     def out_grad(ob, dyf, out):
         for cut in (0, 1):
@@ -909,13 +921,14 @@
     out_grad(ob2, dy2f, goc)
     push_grad(goc, roc, 3)
     gat5.done()
-    relay_grad(gac, rac, 2)
     out_grad(ob1, dy1f, gos)
     push_grad(gos, ros, 5)
     attend_back(qa1, ka1, v1, ot1, lse1, dy1f, wo.at[0], nq, True, dqkv, first3[0], dqkv, first3[1], first3[2])
+    relay_grad(gu, ru, 0)
     rs5 = Scatter(net, plane, pa.at[pl.ds(0, n)], ra.at[pl.ds(0, n)], "sum")
     partial(rs5, flat(dqkv, t), lambda rows: dot_t(rows, wbuf[:, 0:384]), t)
     rs5.fold()
+    relay_grad(gac, rac, 2)
     rse.reduce(into(genc_ref))
     if q == 1:
         back1.wait()

time: 299 us -> 269 us (0.90)
  Pallas kernels: 294 us -> 267 us
    pallas_call x1, Pallas kernels: 291 us -> 263 us  [body(): pl.pallas_call(functools.partial(layer, dims), out_shape=out_shape, in_sp...]
where the time goes in v4:
time: 269 us; the launch traced here: 268 us
  Pallas kernels  267 us (99%)
    pallas_call x1, Pallas kernels, body(): pl.pallas_call(functools.partial(layer, dims), out_shape=out_shape, in_sp...  263 us

profile of v4, /device:TPU:8, one launch (start us, length us, event | category | flops | bytes accessed | tf_op | source)
XLA Modules:
  0.0 267.5 jit_solution(16754131502933972810)
XLA Ops:
  0.6 263.5 %layer.1 = (bf16[128,1024]{1,0:T(8,128)(2,1)}, f32[128,1024]{1,0:T(8,128)}, f32[64,1024]{1,0:T(8,128)}, bf16[8,1,32,1024]{3,2,1,0:T(8,128)(2,1)}, bf16[8,1,32,10...) custom-call(bf16[128,1024]{1,0:T(8,128)(2,1)} %bitcast.3, ...), custom_call_target="tpu_custom_call" | custom-call | flops 20999999488 | bytes 30000000 | tf_op jit(solution)/shard_map/layer/pallas_call | solution.py:1082
  264.1 3.3 %closing.1 = (bf16[1,128,1024]{2,1,0:T(8,128)(2,1)}, f32[1,128,1024]{2,1,0:T(8,128)}, f32[1,64,1024]{2,1,0:T(8,128)}, f32[32,8192]{1,0:T(8,128)}, f32[32,8192]{1...) custom-call(bf16[128,1024]{1,0:T(8,128)(2,1)} %get-tuple-element.17.refs_0_, f32[128,1024]{1,0:T(8,128)} %get-tuple-element.18.refs_1_, ...), custom_call_target="tpu_custom_call" | custom-call | tf_op jit(solution)/shard_map/closing/pallas_call | solution.py:1095

commit v5 on v4

--- a/solution.py
+++ b/solution.py
@@ -532,9 +532,6 @@
     if q == 1:
         away1 = local_copy(n1f, hold1, 10)
 
-    for k in range(4):
-        push_feed(k)
-
     def attend(qa, ka, vt_ref, ot, ob, lse, keys, causal):
         def one(j, _):
             qrows = tile_rows(j)
@@ -630,6 +627,8 @@
     rs1.fold()
     if relayed:
         relay_z(lambda zz: weight_rows(zz, 2), wslots[2])
+    for k in range(4):
+        push_feed(k)
     rs1.reduce(into(x1))
     x1[...] = x_ref[...].astype(f32) + (x1[...] + row(8))
     hat, _ = normed(x1[...])
@@ -789,8 +788,6 @@
     rs3.fold()
     weight_grad(whole(n3f, rows_wide), lambda: du[...], gu, pl.ds(0, fw))
     push_grad(gu, ru, 0)
-    partial(rsm, flat(act, t), lambda rows: dot_t(rows, wdown[...]), t)
-    rsm.fold()
 
     gat3.drain()
     gatg.drain()
@@ -805,7 +802,9 @@
     gat4.start()
     vt[7:8, :] = jnp.sum(dy.astype(f32), axis=0, keepdims=True)
     rs3.drain()
+    partial(rsm, flat(act, t), lambda rows: dot_t(rows, wdown[...]), t)
     gat4.levels()
+    rsm.fold()
     back2 = local_copy(hold2, n2back, 12)
     gat4.done()
 

time: 269 us -> 263 us (0.978)
  Pallas kernels: 267 us -> 261 us
    pallas_call x1, Pallas kernels: 263 us -> 258 us  [body(): pl.pallas_call(functools.partial(layer, dims), out_shape=out_shape, in_sp...]
where the time goes in v5:
time: 263 us; the launch traced here: 262 us
  Pallas kernels  261 us (99%)
    pallas_call x1, Pallas kernels, body(): pl.pallas_call(functools.partial(layer, dims), out_shape=out_shape, in_sp...  258 us

profile of v5, /device:TPU:8, one launch (start us, length us, event | category | flops | bytes accessed | tf_op | source)
XLA Modules:
  0.0 262.0 jit_solution(3934802451089819613)
XLA Ops:
  0.6 258.0 %layer.1 = (bf16[128,1024]{1,0:T(8,128)(2,1)}, f32[128,1024]{1,0:T(8,128)}, f32[64,1024]{1,0:T(8,128)}, bf16[8,1,32,1024]{3,2,1,0:T(8,128)(2,1)}, bf16[8,1,32,10...) custom-call(bf16[128,1024]{1,0:T(8,128)(2,1)} %bitcast.3, ...), custom_call_target="tpu_custom_call" | custom-call | flops 20999999488 | bytes 30000000 | tf_op jit(solution)/shard_map/layer/pallas_call | solution.py:1081
  258.6 3.3 %closing.1 = (bf16[1,128,1024]{2,1,0:T(8,128)(2,1)}, f32[1,128,1024]{2,1,0:T(8,128)}, f32[1,64,1024]{2,1,0:T(8,128)}, f32[32,8192]{1,0:T(8,128)}, f32[32,8192]{1...) custom-call(bf16[128,1024]{1,0:T(8,128)(2,1)} %get-tuple-element.17.refs_0_, f32[128,1024]{1,0:T(8,128)} %get-tuple-element.18.refs_1_, ...), custom_call_target="tpu_custom_call" | custom-call | tf_op jit(solution)/shard_map/closing/pallas_call | solution.py:1094
